TPU v7x, 32 devices: a whole 2x2x4 slice. The times are simulated.
32 devices in a mesh: dp: 8 (over z, core), fsdp: 4 (over y, x).
Axes of the slice: x: 2, y: 2, z: 4, core: 2. Of those that a mesh axis runs over, the one named last changes fastest.
Arguments:
- hidden: bfloat16 [128, 512, 768], P(('dp', 'fsdp')), may hold values from -6 to 6
- lengths: int32 [128], P(('dp', 'fsdp')), may hold values from 40 to 512, as said below
- key_mask: int32 [128, 512], P(('dp', 'fsdp')), may hold values from 0 to 1, as said below
- cotangent: bfloat16 [128, 256, 768], P(('dp', 'fsdp')), may hold values from -6 to 6
- attention_weight: float32 [5, 768, 768], P(None, ('dp', 'fsdp')), may hold values from -0.3125 to 0.3125
- expand_weight: float32 [768, 3072], P(('dp', 'fsdp')), may hold values from -0.21875 to 0.21875
- contract_weight: float32 [3072, 768], P(('dp', 'fsdp')), may hold values from -0.109375 to 0.109375
- small_params: float32 [13, 768], P(None, ('dp', 'fsdp')), may hold values from -1.5 to 1.5, as said below
- mean_attention: float32 [5, 768, 768], P(None, ('dp', 'fsdp')), may hold values from -192 to 192
- mean_expand: float32 [768, 3072], P(('dp', 'fsdp')), may hold values from -192 to 192
- mean_contract: float32 [3072, 768], P(('dp', 'fsdp')), may hold values from -192 to 192
- mean_small: float32 [13, 768], P(None, ('dp', 'fsdp')), may hold values from -192 to 192
- square_attention: float32 [5, 768, 768], P(None, ('dp', 'fsdp')), may hold values from 512 to 8192
- square_expand: float32 [768, 3072], P(('dp', 'fsdp')), may hold values from 512 to 8192
- square_contract: float32 [3072, 768], P(('dp', 'fsdp')), may hold values from 512 to 8192
- square_small: float32 [13, 768], P(None, ('dp', 'fsdp')), may hold values from 512 to 8192
- update_step: int32 [1], replicated, may hold values from 1 to 19
- update_rates: float32 [4], replicated, may hold values from 0.05 to 0.95, as said below
Outputs:
- pooled_out: bfloat16 [128, 256, 768], P(('dp', 'fsdp'))
- input_grad: bfloat16 [128, 512, 768], P(('dp', 'fsdp'))
- attention_grad: float32 [5, 768, 768], P(None, ('dp', 'fsdp'))
- expand_grad: float32 [768, 3072], P(('dp', 'fsdp'))
- contract_grad: float32 [3072, 768], P(('dp', 'fsdp'))
- small_grad: float32 [13, 768], P(None, ('dp', 'fsdp'))
- attention_next: float32 [5, 768, 768], P(None, ('dp', 'fsdp'))
- expand_next: float32 [768, 3072], P(('dp', 'fsdp'))
- contract_next: float32 [3072, 768], P(('dp', 'fsdp'))
- small_next: float32 [13, 768], P(None, ('dp', 'fsdp'))
- attention_mean: float32 [5, 768, 768], P(None, ('dp', 'fsdp'))
- expand_mean: float32 [768, 3072], P(('dp', 'fsdp'))
- contract_mean: float32 [3072, 768], P(('dp', 'fsdp'))
- small_mean: float32 [13, 768], P(None, ('dp', 'fsdp'))
- attention_square: float32 [5, 768, 768], P(None, ('dp', 'fsdp'))
- expand_square: float32 [768, 3072], P(('dp', 'fsdp'))
- contract_square: float32 [3072, 768], P(('dp', 'fsdp'))
- small_square: float32 [13, 768], P(None, ('dp', 'fsdp'))
Inputs may be any that keep to these rules, and one draw needn't show every extreme that they name: `lengths`: in every aligned block of 8 sequences at least one has 512 tokens; every sequence has at least 40. `key_mask`: position 0 of every sequence is 1. `small_params`: rows 4 and 7 lie between 0.55 and 1.45. `update_rates`: learning rate first, then the two moment decays, then weight decay.
All inputs are finite; a program needn't handle non-finite values.
Results may differ from a plain program's by a relative error of at most 0.015.
The roundings to bfloat16 on the way count: a program that leaves them out, or rounds other values in their place, can miss the bound.
Values may be sent and summed in bfloat16 or wider, within the bound.
No kernel may reach another device: no remote copies, remote signals or barrier semaphores. Data moves between devices by JAX's collectives and lax.ppermute only.
A program may use at most 256 MiB of HBM per device.

v0:
```python
import math

import jax
import jax.numpy as jnp
from jax import lax
from jax.sharding import PartitionSpec as P

HEADS = 12
HEAD = 64


EPSILON = 1e-06
SCORE_SCALE = 0.125
MASK_FILL = -1000000000.0


def rel_table(length, width):
    places = length - jnp.arange(2 * length, dtype=jnp.float32)
    half_width = width // 2
    frequency = jnp.exp(
        jnp.arange(half_width, dtype=jnp.float32) * (-2.0 * math.log(10000.0) / width)
    )
    angles = places[:, None] * frequency[None, :]
    return jnp.concatenate([jnp.sin(angles), jnp.cos(angles)], axis=1)


def move_rows(table_scores, toward_end):
    rows_here = table_scores.shape[-2]
    span = table_scores.shape[-1]
    row_index = jnp.arange(rows_here, dtype=jnp.int32)[:, None]
    current = table_scores
    for level in range(max(1, (rows_here - 1).bit_length())):
        amount = 2 << level
        filler = jnp.zeros(current.shape[:-1] + (amount,), current.dtype)
        if toward_end:
            moved = jnp.concatenate([filler, current[..., : span - amount]], axis=-1)
        else:
            moved = jnp.concatenate([current[..., amount:], filler], axis=-1)
        chosen = row_index >> level & 1 == 1
        current = jnp.where(chosen, moved, current)
    return current


def shift_rel(table_scores, length):
    return move_rows(table_scores, True)[..., length:]


def unshift_rel(grad_rows, length):
    leading = grad_rows.shape[:-1]
    widened = jnp.concatenate([jnp.zeros(leading + (length,), grad_rows.dtype), grad_rows], axis=-1)
    return move_rows(widened, False)


def normalize(values):
    center = values - jnp.mean(values, axis=-1, keepdims=True)
    inverse = lax.rsqrt(jnp.mean(center * center, axis=-1, keepdims=True) + EPSILON)
    return (center * inverse, inverse)


def norm_back(grad_norm, normed, inverse):
    return inverse * (
        grad_norm
        - jnp.mean(grad_norm, axis=-1, keepdims=True)
        - normed * jnp.mean(grad_norm * normed, axis=-1, keepdims=True)
    )


def gelu_slope(inputs):
    return (
        0.5 * (1.0 + jax.scipy.special.erf(inputs * 0.7071067811865476))
        + inputs * jnp.exp(-0.5 * inputs * inputs) * 0.3989422804014327
    )


def collect(attention_part, expand_part, contract_part, small_part):
    return (
        lax.all_gather(attention_part, ("dp", "fsdp"), axis=1, tiled=True),
        lax.all_gather(expand_part, ("dp", "fsdp"), axis=0, tiled=True),
        lax.all_gather(contract_part, ("dp", "fsdp"), axis=0, tiled=True),
        lax.all_gather(small_part, ("dp", "fsdp"), axis=1, tiled=True),
    )


def spread(attention_part, expand_part, contract_part, small_part):
    return (
        lax.psum_scatter(attention_part, ("dp", "fsdp"), scatter_dimension=1, tiled=True),
        lax.psum_scatter(expand_part, ("dp", "fsdp"), scatter_dimension=0, tiled=True),
        lax.psum_scatter(contract_part, ("dp", "fsdp"), scatter_dimension=0, tiled=True),
        lax.psum_scatter(small_part, ("dp", "fsdp"), scatter_dimension=1, tiled=True),
    )


def attend_row(content_row, place_row, keys_row, values_row, bias_row, rel_heads, length):
    pooled_len = content_row.shape[0]
    content_heads = content_row.reshape(pooled_len, HEADS, HEAD)
    place_heads = place_row.reshape(pooled_len, HEADS, HEAD)
    keys_heads = keys_row.reshape(length, HEADS, HEAD)
    values_heads = values_row.reshape(length, HEADS, HEAD)
    content = jnp.einsum(
        "phe,she->hps", content_heads, keys_heads, preferred_element_type=jnp.float32
    )
    placed = jnp.einsum("phe,mhe->hpm", place_heads, rel_heads, preferred_element_type=jnp.float32)
    scores = (content + shift_rel(placed, length)) * SCORE_SCALE + bias_row[None, None, :]
    top = jnp.max(scores, axis=-1, keepdims=True)
    total = jnp.sum(jnp.exp(scores - top), axis=-1, keepdims=True)
    row_lse = top + jnp.log(total)
    probs_low = jnp.exp(scores - row_lse).astype(jnp.bfloat16)
    context = jnp.einsum(
        "hps,she->phe", probs_low, values_heads, preferred_element_type=jnp.float32
    )
    return (context.reshape(pooled_len, HEADS * HEAD).astype(jnp.bfloat16), row_lse[:, :, 0])


def attend_back(
    content_row, place_row, keys_row, values_row, bias_row, lse_row, dctx_row, rel_heads, length
):
    pooled_len = content_row.shape[0]
    width = HEADS * HEAD
    content_heads = content_row.reshape(pooled_len, HEADS, HEAD)
    place_heads = place_row.reshape(pooled_len, HEADS, HEAD)
    keys_heads = keys_row.reshape(length, HEADS, HEAD)
    values_heads = values_row.reshape(length, HEADS, HEAD)
    dctx_heads = dctx_row.reshape(pooled_len, HEADS, HEAD)
    content = jnp.einsum(
        "phe,she->hps", content_heads, keys_heads, preferred_element_type=jnp.float32
    )
    placed = jnp.einsum("phe,mhe->hpm", place_heads, rel_heads, preferred_element_type=jnp.float32)
    scores = (content + shift_rel(placed, length)) * SCORE_SCALE + bias_row[None, None, :]
    probs = jnp.exp(scores - lse_row[:, :, None])
    probs_low = probs.astype(jnp.bfloat16)
    grad_probs = jnp.einsum(
        "phe,she->hps", dctx_heads, values_heads, preferred_element_type=jnp.float32
    )
    grad_values = jnp.einsum(
        "hps,phe->she", probs_low, dctx_heads, preferred_element_type=jnp.float32
    )
    grad_scores = probs * (grad_probs - jnp.sum(probs * grad_probs, axis=-1, keepdims=True))
    grad_raw = (grad_scores * SCORE_SCALE).astype(jnp.bfloat16)
    grad_content = jnp.einsum(
        "hps,she->phe", grad_raw, keys_heads, preferred_element_type=jnp.float32
    )
    grad_keys = jnp.einsum(
        "hps,phe->she", grad_raw, content_heads, preferred_element_type=jnp.float32
    )
    grad_table = unshift_rel(grad_raw, length)
    grad_place = jnp.einsum(
        "hpm,mhe->phe", grad_table, rel_heads, preferred_element_type=jnp.float32
    )
    grad_rel = jnp.einsum(
        "hpm,phe->mhe", grad_table, place_heads, preferred_element_type=jnp.float32
    )
    return (
        grad_content.reshape(pooled_len, width),
        grad_place.reshape(pooled_len, width),
        grad_keys.reshape(length, width),
        grad_values.reshape(length, width),
        grad_rel,
    )


def adamw(weight, moment, second, gradient, step_value, rates):
    new_moment = rates[1] * moment + (1.0 - rates[1]) * gradient
    new_second = rates[2] * second + (1.0 - rates[2]) * gradient * gradient
    moment_hat = new_moment / (1.0 - jnp.power(rates[1], step_value))
    second_hat = new_second / (1.0 - jnp.power(rates[2], step_value))
    new_weight = weight - rates[0] * (
        moment_hat / (jnp.sqrt(second_hat) + 1e-08) + rates[3] * weight
    )
    return (new_weight, new_moment, new_second)


def shards(
    hidden,
    lengths,
    key_mask,
    cotangent,
    attention_weight,
    expand_weight,
    contract_weight,
    small_params,
    mean_attention,
    mean_expand,
    mean_contract,
    mean_small,
    square_attention,
    square_expand,
    square_contract,
    square_small,
    update_step,
    update_rates,
):
    batch_rows, length, width = hidden.shape
    pooled_len = length // 2
    positions = jnp.arange(length, dtype=jnp.int32)
    valid_keys = (key_mask == 1) & (positions[None, :] < lengths[:, None])
    key_bias = jnp.where(valid_keys, 0.0, MASK_FILL).astype(jnp.float32)
    pooled_mask = jnp.max(valid_keys.astype(jnp.float32).reshape(batch_rows, pooled_len, 2), axis=2)
    table_low = rel_table(length, width).astype(jnp.bfloat16)
    attention_low = attention_weight.astype(jnp.bfloat16)
    expand_low = expand_weight.astype(jnp.bfloat16)
    contract_low = contract_weight.astype(jnp.bfloat16)
    small_low = small_params.astype(jnp.bfloat16)
    att_full, expand_full, contract_full, small_full = collect(
        attention_low, expand_low, contract_low, small_low
    )
    small_vals = small_full.astype(jnp.float32)
    pair = hidden.astype(jnp.float32).reshape(batch_rows, pooled_len, 2, width)
    pooled = (pair[:, :, 0] + pair[:, :, 1]) * 0.5
    pooled_low = pooled.astype(jnp.bfloat16)
    query = jnp.einsum("bpd,de->bpe", pooled_low, att_full[0], preferred_element_type=jnp.float32)
    query_content = (query + small_vals[0]).astype(jnp.bfloat16)
    query_place = (query + small_vals[1]).astype(jnp.bfloat16)
    keys_low = jnp.einsum(
        "bsd,de->bse", hidden, att_full[1], preferred_element_type=jnp.float32
    ).astype(jnp.bfloat16)
    values_low = (
        jnp.einsum("bsd,de->bse", hidden, att_full[2], preferred_element_type=jnp.float32)
        + small_vals[2]
    ).astype(jnp.bfloat16)
    rel_heads = (
        jnp.dot(table_low, att_full[3], preferred_element_type=jnp.float32)
        .astype(jnp.bfloat16)
        .reshape(2 * length, HEADS, HEAD)
    )

    def forward_row(carry, row_inputs):
        context_row, lse_row = attend_row(
            row_inputs[0],
            row_inputs[1],
            row_inputs[2],
            row_inputs[3],
            row_inputs[4],
            rel_heads,
            length,
        )
        return (carry, (context_row, lse_row))

    unused, (context_low, row_lse) = lax.scan(
        forward_row,
        jnp.zeros((), jnp.float32),
        (query_content, query_place, keys_low, values_low, key_bias),
    )
    branch = (
        jnp.einsum("bpe,ed->bpd", context_low, att_full[4], preferred_element_type=jnp.float32)
        + small_vals[3]
    )
    first_norm, first_inv = normalize(pooled + branch)
    first_out = first_norm * small_vals[4] + small_vals[5]
    first_low = first_out.astype(jnp.bfloat16)
    inner = jnp.einsum(
        "bpd,df->bpf", first_low, expand_full, preferred_element_type=jnp.float32
    ) + small_vals[9:].reshape(-1)
    inner_low = jax.nn.gelu(inner, approximate=False).astype(jnp.bfloat16)
    second_sum = (
        first_out
        + jnp.einsum("bpf,fd->bpd", inner_low, contract_full, preferred_element_type=jnp.float32)
        + small_vals[6]
    )
    second_norm, second_inv = normalize(second_sum)
    result = (second_norm * small_vals[7] + small_vals[8]) * pooled_mask[:, :, None]
    pooled_out = result.astype(jnp.bfloat16)
    later = lax.optimization_barrier(
        ((attention_low, expand_low, contract_low, small_low), result)
    )[0]
    att_full, expand_full, contract_full, small_full = collect(
        later[0], later[1], later[2], later[3]
    )
    grad_out = cotangent.astype(jnp.float32) * pooled_mask[:, :, None]
    grad_gain_two = jnp.sum(grad_out * second_norm, axis=(0, 1))
    grad_shift_two = jnp.sum(grad_out, axis=(0, 1))
    grad_second = norm_back(grad_out * small_vals[7], second_norm, second_inv)
    grad_contract_bias = jnp.sum(grad_second, axis=(0, 1))
    second_low = grad_second.astype(jnp.bfloat16)
    grad_contract = jnp.einsum(
        "bpf,bpd->fd", inner_low, second_low, preferred_element_type=jnp.float32
    )
    grad_inner = jnp.einsum(
        "bpd,fd->bpf", second_low, contract_full, preferred_element_type=jnp.float32
    ) * gelu_slope(inner)
    grad_expand_bias = jnp.sum(grad_inner, axis=(0, 1))
    grad_inner_low = grad_inner.astype(jnp.bfloat16)
    grad_expand = jnp.einsum(
        "bpd,bpf->df", first_low, grad_inner_low, preferred_element_type=jnp.float32
    )
    grad_first_out = grad_second + jnp.einsum(
        "bpf,df->bpd", grad_inner_low, expand_full, preferred_element_type=jnp.float32
    )
    grad_gain_one = jnp.sum(grad_first_out * first_norm, axis=(0, 1))
    grad_shift_one = jnp.sum(grad_first_out, axis=(0, 1))
    grad_first = norm_back(grad_first_out * small_vals[4], first_norm, first_inv)
    grad_out_bias = jnp.sum(grad_first, axis=(0, 1))
    grad_first_low = grad_first.astype(jnp.bfloat16)
    grad_output_proj = jnp.einsum(
        "bpe,bpd->ed", context_low, grad_first_low, preferred_element_type=jnp.float32
    )
    grad_context = jnp.einsum(
        "bpd,ed->bpe", grad_first_low, att_full[4], preferred_element_type=jnp.float32
    ).astype(jnp.bfloat16)

    def backward_row(total, row_inputs):
        pieces = attend_back(
            row_inputs[0],
            row_inputs[1],
            row_inputs[2],
            row_inputs[3],
            row_inputs[4],
            row_inputs[5],
            row_inputs[6],
            rel_heads,
            length,
        )
        return (total + pieces[4], (pieces[0], pieces[1], pieces[2], pieces[3]))

    rel_start = jnp.zeros((2 * length, HEADS, HEAD), jnp.float32)
    grad_rel_heads, (grad_qc, grad_qp, grad_keys_all, grad_values_all) = lax.scan(
        backward_row,
        rel_start,
        (query_content, query_place, keys_low, values_low, key_bias, row_lse, grad_context),
    )
    grad_content_bias = jnp.sum(grad_qc, axis=(0, 1))
    grad_place_bias = jnp.sum(grad_qp, axis=(0, 1))
    grad_query_low = (grad_qc + grad_qp).astype(jnp.bfloat16)
    grad_query = jnp.einsum(
        "bpd,bpe->de", pooled_low, grad_query_low, preferred_element_type=jnp.float32
    )
    grad_pooled = grad_first + jnp.einsum(
        "bpe,de->bpd", grad_query_low, att_full[0], preferred_element_type=jnp.float32
    )
    grad_keys_low = grad_keys_all.astype(jnp.bfloat16)
    grad_key = jnp.einsum("bsd,bse->de", hidden, grad_keys_low, preferred_element_type=jnp.float32)
    grad_value_bias = jnp.sum(grad_values_all, axis=(0, 1))
    grad_values_low = grad_values_all.astype(jnp.bfloat16)
    grad_value = jnp.einsum(
        "bsd,bse->de", hidden, grad_values_low, preferred_element_type=jnp.float32
    )
    grad_rel = jnp.dot(
        table_low.astype(jnp.float32).T,
        grad_rel_heads.reshape(2 * length, width),
        precision=lax.Precision.HIGHEST,
        preferred_element_type=jnp.float32,
    )
    unpooled = jnp.broadcast_to(
        (grad_pooled * 0.5)[:, :, None, :], (batch_rows, pooled_len, 2, width)
    ).reshape(batch_rows, length, width)
    grad_hidden = (
        unpooled
        + jnp.einsum("bse,de->bsd", grad_keys_low, att_full[1], preferred_element_type=jnp.float32)
        + jnp.einsum(
            "bse,de->bsd", grad_values_low, att_full[2], preferred_element_type=jnp.float32
        )
    )
    input_grad = grad_hidden.astype(jnp.bfloat16)
    grad_attention = jnp.stack([grad_query, grad_key, grad_value, grad_rel, grad_output_proj])
    grad_small = jnp.concatenate(
        [
            jnp.stack(
                [
                    grad_content_bias,
                    grad_place_bias,
                    grad_value_bias,
                    grad_out_bias,
                    grad_gain_one,
                    grad_shift_one,
                    grad_contract_bias,
                    grad_gain_two,
                    grad_shift_two,
                ]
            ),
            grad_expand_bias.reshape(-1, width),
        ],
        axis=0,
    )
    attention_grad, expand_grad, contract_grad, small_grad = spread(
        grad_attention, grad_expand, grad_contract, grad_small
    )
    step_value = update_step[0].astype(jnp.float32)
    attention_next, attention_mean, attention_square = adamw(
        attention_weight, mean_attention, square_attention, attention_grad, step_value, update_rates
    )
    expand_next, expand_mean, expand_square = adamw(
        expand_weight, mean_expand, square_expand, expand_grad, step_value, update_rates
    )
    contract_next, contract_mean, contract_square = adamw(
        contract_weight, mean_contract, square_contract, contract_grad, step_value, update_rates
    )
    small_next, small_mean, small_square = adamw(
        small_params, mean_small, square_small, small_grad, step_value, update_rates
    )
    return (
        pooled_out,
        input_grad,
        attention_grad,
        expand_grad,
        contract_grad,
        small_grad,
        attention_next,
        expand_next,
        contract_next,
        small_next,
        attention_mean,
        expand_mean,
        contract_mean,
        small_mean,
        attention_square,
        expand_square,
        contract_square,
        small_square,
    )


def solution(mesh):
    in_specs = (
        P(("dp", "fsdp"), None, None),
        P(("dp", "fsdp")),
        P(("dp", "fsdp"), None),
        P(("dp", "fsdp"), None, None),
        P(None, ("dp", "fsdp"), None),
        P(("dp", "fsdp"), None),
        P(("dp", "fsdp"), None),
        P(None, ("dp", "fsdp")),
        P(None, ("dp", "fsdp"), None),
        P(("dp", "fsdp"), None),
        P(("dp", "fsdp"), None),
        P(None, ("dp", "fsdp")),
        P(None, ("dp", "fsdp"), None),
        P(("dp", "fsdp"), None),
        P(("dp", "fsdp"), None),
        P(None, ("dp", "fsdp")),
        P(),
        P(),
    )
    out_specs = (
        P(("dp", "fsdp"), None, None),
        P(("dp", "fsdp"), None, None),
        P(None, ("dp", "fsdp"), None),
        P(("dp", "fsdp"), None),
        P(("dp", "fsdp"), None),
        P(None, ("dp", "fsdp")),
        P(None, ("dp", "fsdp"), None),
        P(("dp", "fsdp"), None),
        P(("dp", "fsdp"), None),
        P(None, ("dp", "fsdp")),
        P(None, ("dp", "fsdp"), None),
        P(("dp", "fsdp"), None),
        P(("dp", "fsdp"), None),
        P(None, ("dp", "fsdp")),
        P(None, ("dp", "fsdp"), None),
        P(("dp", "fsdp"), None),
        P(("dp", "fsdp"), None),
        P(None, ("dp", "fsdp")),
    )
    return jax.shard_map(shards, mesh=mesh, in_specs=in_specs, out_specs=out_specs, check_vma=False)
```

profile of v0, /device:TPU:0, one launch (start us, length us, event | category | flops | bytes accessed | tf_op | source)
XLA Modules:
  0.0 1654.8 jit_solution(5892233123698493555)
XLA Ops:
  13.3 71.2 %all-gather = bf16[32,24,13]{1,2,0:T(8,128)(2,1)S(1)} all-gather(bf16[1,24,13]{1,2,0:T(8,128)(2,1)S(1)} %convert_bitcast_fusion), channel_id=1, replica_groups=mesh['dp'=8,'fsdp'=4] {'dp','fsdp'}, dimensions={0}, use_global_device_ids=true | all-gather | bytes 20592 | tf_op jit(solution)/shard_map/all_gather | solution.py:80
  136.2 259.7 %while.31 = (s32[]{:T(128)}, bf16[4,256,768]{1,2,0:T(8,128)(2,1)}, f32[4,12,256]{2,1,0:T(8,128)}, bf16[4,512,768]{1,2,0:T(8,128)(2,1)}, bf16[4,256,768]{1,2,0:T(...) while((s32[]{:T(128)}, bf16[4,256,768]{1,2,0:T(8,128)(2,1)}, ...), condition=%wide.region_3.4_spmd, body=%wide.region_0.3_spmd.sunk | while | flops 841681920 | bytes 387455232 | solution.py:238
  177.2 11.5 pad_select_fusion.53
  242.3 11.5 pad_select_fusion.53
  307.0 11.5 pad_select_fusion.53
  371.6 11.5 pad_select_fusion.53
  404.2 12.5 fusion.48
  421.2 29.9 %fusion.22 = bf16[4,256,3072]{2,1,0:T(8,128)(2,1)} fusion(f32[4,256,3072]{2,1,0:T(8,128)S(1)} %get-tuple-element.400, f32[3072]{0:T(1024)S(1)} %copy-done.76, u8[256,3072]{1,0:T(8,128)(4,1)S(1)} %get-tuple-element.293, u8[256,3072]{1,0:T(8,128)(4,1)S(1)} %get-tuple-element.292), kind=kLoop, calls=%fused_computation.86 | loop fusion | flops 223346688 | bytes 20459520 | tf_op jit(solution)/shard_map/convert_element_type | solution.py:253
  468.2 12.5 convolution_bitcast_fusion
  480.8 42.8 %all-gather.14.cloned.1.call-done = bf16[3072,768]{1,0:T(8,128)(2,1)} async-done(((bf16[96,768]{1,0:T(8,128)(2,1)}), bf16[3072,768]{1,0:T(8,128)(2,1)}) %all-gather.14.cloned.1.call-update) | async-done | bytes 4718608 | tf_op jit(solution)/shard_map/all_gather | solution.py:79
  523.6 15.1 fusion.96
  538.6 50.6 %all-gather.16.cloned.1.call-done = bf16[768,3072]{1,0:T(8,128)(2,1)} async-done(((bf16[24,3072]{1,0:T(8,128)(2,1)}), bf16[768,3072]{1,0:T(8,128)(2,1)}) %all-gather.16.cloned.1.call-update) | async-done | bytes 4718608 | tf_op jit(solution)/shard_map/all_gather | solution.py:78
  589.3 12.8 multiply_reduce_fusion.2
  615.7 43.4 %all-gather.18.cloned.1.call-done = bf16[5,768,768]{2,1,0:T(8,128)(2,1)} async-done(((bf16[5,24,768]{2,1,0:T(8,128)(2,1)}), bf16[5,768,768]{2,1,0:T(8,128)(2,1)}) %all-gather.18.cloned.1.call-update) | async-done | bytes 5898256 | tf_op jit(solution)/shard_map/all_gather | solution.py:77
  663.9 805.4 %while.32 = (s32[]{:T(128)}, f32[1024,12,64]{0,2,1:T(8,128)}, f32[4,256,768]{1,2,0:T(8,128)}, f32[4,256,768]{1,2,0:T(8,128)}, bf16[4,512,768]{1,2,0:T(8,128)(2,1...) while((s32[]{:T(128)}, f32[1024,12,64]{0,2,1:T(8,128)}, ...), condition=%wide.region_15.16_spmd.clone, body=%wide.region_13.15_spmd.clone.sunk | while | flops 2485134848 | bytes 854266688 | solution.py:315
  710.2 11.5 pad_select_fusion.62
  785.3 9.6 slice.348
  803.8 9.6 slice.349
  822.7 9.8 slice.350
  911.3 11.5 pad_select_fusion.62
  986.3 9.4 slice.348
  1004.7 9.6 slice.349
  1023.3 9.5 slice.350
  1110.0 11.4 pad_select_fusion.62
  1184.6 9.4 slice.348
  1203.0 9.6 slice.349
  1221.6 9.5 slice.350
  1308.3 11.4 pad_select_fusion.62
  1401.4 9.6 slice.349
  1420.0 9.5 slice.350
  1524.0 41.7 %all-reduce.25 = f32[13,768]{1,0:T(8,128)S(1)} all-reduce(f32[13,768]{1,0:T(8,128)S(1)} %concatenate.83), channel_id=5, replica_groups=mesh['dp'=8,'fsdp'=4] {'dp','fsdp'}, use_global_device_ids=true, to_apply=%region_29.30.clone | all-reduce | flops 9984 | bytes 79872
  1591.3 52.1 %reduce-scatter.5.cloned.1.call-done = f32[5,24,768]{2,1,0:T(8,128)} async-done(((f32[5,768,768]{2,1,0:T(8,128)}), f32[5,24,768]{2,1,0:T(8,128)}) %reduce-scatter.5.cloned.1.call-update) | async-done | bytes 368656 | tf_op jit(solution)/shard_map/reduce_scatter | solution.py:86
  (814 shorter events, 1041.6 us)
Async XLA Ops:
  7.2 81.0 %copy-start.36 = (bf16[4,512,768]{2,1,0:T(8,128)(2,1)S(1)}, bf16[4,512,768]{2,1,0:T(8,128)(2,1)}, u32[]{:S(2)}) copy-start(bf16[4,512,768]{2,1,0:T(8,128)(2,1)} %param.22) | copy-start | bytes 9437188
  7.2 93.4 %all-gather.8.cloned.1.call-start = ((), (), s32[]{:S(2)}) async-start(), calls=%async_computation.3 | async-start | bytes 6082560 | tf_op jit(solution)/shard_map/all_gather | solution.py:77
  9.1 395.1 %all-gather.10.cloned.1.call-start = ((), (), s32[]{:S(2)}) async-start(), calls=%async_computation.4 | async-start | bytes 4866048 | tf_op jit(solution)/shard_map/all_gather | solution.py:78
  10.8 440.3 %all-gather.12.cloned.1.call-start = ((), (), s32[]{:S(2)}) async-start(), calls=%async_computation.5 | async-start | bytes 4866048 | tf_op jit(solution)/shard_map/all_gather | solution.py:79
  12.5 511.0 %all-gather.14.cloned.1.call-start = ((), (), s32[]{:S(2)}) async-start(), calls=%async_computation.6 | async-start | bytes 4866048 | tf_op jit(solution)/shard_map/all_gather | solution.py:79
  136.2 259.7 %copy-start.53 = (f32[768]{0:T(1024)S(1)}, f32[768]{0:T(1024)}, u32[]{:S(2)}) copy-start(f32[768]{0:T(1024)} %get-tuple-element.308) | copy-start | bytes 9220
  460.5 128.8 %copy-start.54 = (f32[4,256]{1,0:T(4,128)}, f32[4,256]{1,0:T(4,128)S(1)}, u32[]{:S(2)}) copy-start(f32[4,256]{1,0:T(4,128)S(1)} %broadcast_multiply_fusion.4) | copy-start | bytes 12292
  461.0 128.2 %copy-start.62 = (f32[4,256]{1,0:T(4,128)}, f32[4,256]{1,0:T(4,128)S(1)}, u32[]{:S(2)}) copy-start(f32[4,256]{1,0:T(4,128)S(1)} %add_rsqrt_fusion) | copy-start | bytes 12292
  464.0 125.3 %all-gather.16.cloned.1.call-start = ((), (), s32[]{:S(2)}) async-start(), calls=%async_computation.7 | async-start | bytes 4866048 | tf_op jit(solution)/shard_map/all_gather | solution.py:78
  464.6 194.6 %all-gather.18.cloned.1.call-start = ((), (), s32[]{:S(2)}) async-start(), calls=%async_computation.8 | async-start | bytes 6082560 | tf_op jit(solution)/shard_map/all_gather | solution.py:77
  465.1 1117.0 %reduce-scatter.9.cloned.1.call-start = ((), (), s32[]{:S(2)}) async-start(), calls=%async_computation.11 | async-start | bytes 9732096 | tf_op jit(solution)/shard_map/reduce_scatter | solution.py:88
  468.1 121.1 %copy-start.80 = (f32[4,256]{1,0:T(4,128)}, f32[4,256]{1,0:T(4,128)S(1)}, u32[]{:S(2)}) copy-start(f32[4,256]{1,0:T(4,128)S(1)} %get-tuple-element.406) | copy-start | bytes 12292
  468.2 121.1 %copy-start.82 = (f32[4,256]{1,0:T(4,128)}, f32[4,256]{1,0:T(4,128)S(1)}, u32[]{:S(2)}) copy-start(f32[4,256]{1,0:T(4,128)S(1)} %get-tuple-element.407) | copy-start | bytes 12292
  480.7 1106.0 %reduce-scatter.7.cloned.1.call-start = ((), (), s32[]{:S(2)}) async-start(), calls=%async_computation.10 | async-start | bytes 9732096 | tf_op jit(solution)/shard_map/reduce_scatter | solution.py:87
  610.6 1032.8 %reduce-scatter.5.cloned.1.call-start = ((), (), s32[]{:S(2)}) async-start(), calls=%async_computation.9 | async-start | bytes 12165120 | tf_op jit(solution)/shard_map/reduce_scatter | solution.py:86
  664.5 45.7 %copy-start.64 = (pred[256]{0:T(512)(128)(4,1)}, pred[256]{0:T(512)(128)(4,1)S(1)}, u32[]{:S(2)}) copy-start(pred[256]{0:T(512)(128)(4,1)S(1)} %and_compare_fusion.46) | copy-start | bytes 772 | tf_op jit(solution)/shard_map/while
  664.5 35.7 %copy-start.66 = (pred[256]{0:T(512)(128)(4,1)}, pred[256]{0:T(512)(128)(4,1)S(1)}, u32[]{:S(2)}) copy-start(pred[256]{0:T(512)(128)(4,1)S(1)} %and_compare_fusion.45) | copy-start | bytes 772 | tf_op jit(solution)/shard_map/while
  664.5 30.8 %copy-start.68 = (pred[256]{0:T(512)(128)(4,1)}, pred[256]{0:T(512)(128)(4,1)S(1)}, u32[]{:S(2)}) copy-start(pred[256]{0:T(512)(128)(4,1)S(1)} %and_compare_fusion.44) | copy-start | bytes 772 | tf_op jit(solution)/shard_map/while
  865.6 45.7 %copy-start.64 = (pred[256]{0:T(512)(128)(4,1)}, pred[256]{0:T(512)(128)(4,1)S(1)}, u32[]{:S(2)}) copy-start(pred[256]{0:T(512)(128)(4,1)S(1)} %and_compare_fusion.46) | copy-start | bytes 772 | tf_op jit(solution)/shard_map/while
  865.6 35.7 %copy-start.66 = (pred[256]{0:T(512)(128)(4,1)}, pred[256]{0:T(512)(128)(4,1)S(1)}, u32[]{:S(2)}) copy-start(pred[256]{0:T(512)(128)(4,1)S(1)} %and_compare_fusion.45) | copy-start | bytes 772 | tf_op jit(solution)/shard_map/while
  865.6 30.8 %copy-start.68 = (pred[256]{0:T(512)(128)(4,1)}, pred[256]{0:T(512)(128)(4,1)S(1)}, u32[]{:S(2)}) copy-start(pred[256]{0:T(512)(128)(4,1)S(1)} %and_compare_fusion.44) | copy-start | bytes 772 | tf_op jit(solution)/shard_map/while
  1064.4 45.7 %copy-start.64 = (pred[256]{0:T(512)(128)(4,1)}, pred[256]{0:T(512)(128)(4,1)S(1)}, u32[]{:S(2)}) copy-start(pred[256]{0:T(512)(128)(4,1)S(1)} %and_compare_fusion.46) | copy-start | bytes 772 | tf_op jit(solution)/shard_map/while
  1064.4 35.7 %copy-start.66 = (pred[256]{0:T(512)(128)(4,1)}, pred[256]{0:T(512)(128)(4,1)S(1)}, u32[]{:S(2)}) copy-start(pred[256]{0:T(512)(128)(4,1)S(1)} %and_compare_fusion.45) | copy-start | bytes 772 | tf_op jit(solution)/shard_map/while
  1262.7 45.7 %copy-start.64 = (pred[256]{0:T(512)(128)(4,1)}, pred[256]{0:T(512)(128)(4,1)S(1)}, u32[]{:S(2)}) copy-start(pred[256]{0:T(512)(128)(4,1)S(1)} %and_compare_fusion.46) | copy-start | bytes 772 | tf_op jit(solution)/shard_map/while
  1262.7 35.7 %copy-start.66 = (pred[256]{0:T(512)(128)(4,1)}, pred[256]{0:T(512)(128)(4,1)S(1)}, u32[]{:S(2)}) copy-start(pred[256]{0:T(512)(128)(4,1)S(1)} %and_compare_fusion.45) | copy-start | bytes 772 | tf_op jit(solution)/shard_map/while
  1515.2 50.6 %copy-start.77 = (f32[13,24]{1,0:T(8,128)S(1)}, f32[13,24]{1,0:T(8,128)}, u32[]{:S(2)}) copy-start(f32[13,24]{1,0:T(8,128)} %param.29) | copy-start | bytes 3748
  1515.2 50.6 %copy-start.85 = (f32[13,24]{1,0:T(8,128)S(1)}, f32[13,24]{1,0:T(8,128)}, u32[]{:S(2)}) copy-start(f32[13,24]{1,0:T(8,128)} %param.37) | copy-start | bytes 3748
  1515.2 50.6 %copy-start.86 = (f32[13,24]{1,0:T(8,128)S(1)}, f32[13,24]{1,0:T(8,128)}, u32[]{:S(2)}) copy-start(f32[13,24]{1,0:T(8,128)} %param.33) | copy-start | bytes 3748
  1524.0 50.0 %slice-start.3 = ((s8[6291456]{0:T(1024)(128)(4,1)}), s8[2097152]{0:T(1024)(128)(4,1)S(1)}, s32[]{:S(2)}) async-start(s8[6291456]{0:T(1024)(128)(4,1)} %bitcast.329), calls=%async_computation.15 | async-start | bytes 4194304
  1582.1 61.3 %copy-start.40 = (f32[5,24,768]{2,1,0:T(8,128)S(1)}, f32[5,24,768]{2,1,0:T(8,128)}, u32[]{:S(2)}) copy-start(f32[5,24,768]{2,1,0:T(8,128)} %param.26) | copy-start | bytes 1105924
  1582.1 61.3 %copy-start.48 = (f32[5,24,768]{2,1,0:T(8,128)S(1)}, f32[5,24,768]{2,1,0:T(8,128)}, u32[]{:S(2)}) copy-start(f32[5,24,768]{2,1,0:T(8,128)} %param.34) | copy-start | bytes 1105924
  1582.1 61.3 %copy-start.49 = (f32[5,24,768]{2,1,0:T(8,128)S(1)}, f32[5,24,768]{2,1,0:T(8,128)}, u32[]{:S(2)}) copy-start(f32[5,24,768]{2,1,0:T(8,128)} %param.30) | copy-start | bytes 1105924
  (193 other events, 1263.9 us)
Sparse Core Ops, SparseCore 0:
  11.5 71.0 all-gather.7
  86.0 62.6 all-gather.9
  152.1 62.3 all-gather.11
  464.1 59.4 all-gather.13
  526.9 62.3 all-gather.15
  592.5 66.5 all-gather.17
  665.6 134.3 reduce-scatter.8
  807.5 134.7 reduce-scatter.6
  1496.0 147.3 reduce-scatter.4
where the time goes:
time: 1670 us; the launch traced here: 1650 us
  other arithmetic  635 us (38%)
  local copies, waits for them, and re-layouts  421 us (25%)
  matrix products  263 us (16%)
  waiting for transfers between devices  190 us (11%)
  blocking collectives  113 us (7%)
  between operations  18.3 us (1%)
    select_n x84, other arithmetic, move_rows(): current = jnp.where(chosen, moved, current)  544 us
    slice x36, local copies, waits for them, and re-layouts, move_rows(): moved = jnp.concatenate([current[..., amount:], filler], axis=-1)  197 us
    slice x24, local copies, waits for them, and re-layouts, move_rows(): moved = jnp.concatenate([filler, current[..., :span - amount]], axis=-1)  74.9 us
    all_gather x1, blocking collectives, collect(): lax.all_gather(small_part, ('dp', 'fsdp'), axis=1, tiled=True)  71.2 us
    reduce_scatter x1, waiting for transfers between devices, spread(): lax.psum_scatter(attention_part, ('dp', 'fsdp'), scatter_dimension=1, til...  52.1 us
    all_gather x2, waiting for transfers between devices, collect(): lax.all_gather(expand_part, ('dp', 'fsdp'), axis=0, tiled=True)  50.7 us
    dynamic_slice x40, local copies, waits for them, and re-layouts, shards(): lax.scan(forward_row, jnp.zeros((), jnp.float32), (query_content, query_p...  50.6 us
    all_gather x2, waiting for transfers between devices, collect(): lax.all_gather(attention_part, ('dp', 'fsdp'), axis=1, tiled=True)  43.4 us
  transfers between devices with their start and end apart: 9, of which 4 were waited for; matrix products, arithmetic and copies ran while one was open for 74% of the time, Pallas kernels for 0%

commit v1 on v0

v1 whole, which is shorter than its diff:
```python
import functools
import math

import jax
import jax.numpy as jnp
from jax import lax
from jax.experimental import pallas as pl
from jax.experimental.pallas import tpu as pltpu
from jax.sharding import PartitionSpec as P

HEAD = 64
GC = 256
GH = GC // HEAD
FC = 768
EPSILON = 1e-06
MASK_FILL = -1000000000.0
ALL = ("dp", "fsdp")
F32 = jnp.float32
BF = jnp.bfloat16
VMEM = 58 << 20
NT = (((1,), (1,)), ((), ()))
TN = (((0,), (0,)), ((), ()))


def dot(a, b):
    return jnp.dot(a, b, preferred_element_type=F32)


def dot_nt(a, b):
    return lax.dot_general(a, b, NT, preferred_element_type=F32)


def dot_tn(a, b):
    return lax.dot_general(a, b, TN, preferred_element_type=F32)


def sds(shape, dtype):
    return jax.ShapeDtypeStruct(shape, dtype)


def seqs(*tail):
    return pl.BlockSpec((1,) + tail, lambda s, *_: (s,) + (0,) * len(tail))


def whole(*shape):
    return pl.BlockSpec(shape, lambda *_: (0,) * len(shape), pipeline_mode=pl.Buffered(1))


def params():
    return pltpu.CompilerParams(vmem_limit_bytes=VMEM)


def cost(macs, moved, exps=0):
    return pl.CostEstimate(flops=int(2 * macs), bytes_accessed=int(moved), transcendentals=int(exps))


def rel_table(length, width):
    places = length - jnp.arange(2 * length, dtype=F32)
    half_width = width // 2
    frequency = jnp.exp(jnp.arange(half_width, dtype=F32) * (-2.0 * math.log(10000.0) / width))
    angles = places[:, None] * frequency[None, :]
    return jnp.concatenate([jnp.sin(angles), jnp.cos(angles)], axis=1)


X, Y, CORE, Z = 1, 2, 4, 8
HALVES = ((X, Y), (Y, X))


def pairs(bit):
    return [(d, d ^ bit) for d in range(32)]


def swap(a, bit):
    return lax.ppermute(a, ALL, pairs(bit))


def flat_of(rel, half):
    low, high = HALVES[half]
    return (rel & 3) * Z + (rel >> 2 & 1) * low + (rel >> 3 & 1) * high + (rel >> 4 & 1) * CORE


def after(x, *earlier):
    return lax.optimization_barrier((x, earlier))[0]


def assemble_kernel(stacked, me_ref, *refs):
    ins, outs = refs[:8], refs[8:]
    for half in range(2):
        for rel in range(32):
            k = jnp.bitwise_xor(me_ref[0], flat_of(rel, half))
            src = ins[4 * half + rel // 8]
            n, r = src.shape[1], src.shape[2]
            for i in range(n):
                if stacked:
                    outs[half][i, k] = src[rel % 8, i]
                else:
                    outs[0][k, half * r : (half + 1) * r, :] = src[rel % 8, i]


def gather(me, part, split, stacked=True, gate=None):
    n, r, c = part.shape
    along = [part] + [swap(part, k * Z) for k in range(1, 4)]
    halves = [jnp.stack([p[:split] for p in along]), jnp.stack([p[split:] for p in along])]
    token = halves[0]
    firsts = [jnp.concatenate([h, swap(h, HALVES[i][0])], axis=0) for i, h in enumerate(halves)]
    seconds = [swap(h, HALVES[i][1]) for i, h in enumerate(firsts)]
    ins = []
    for f, s in zip(firsts, seconds):
        ins += [f, s, swap(f, CORE), swap(s, CORE)]
    shapes = [(split, 32, r, c), (n - split, 32, r, c)] if stacked else [(32, n * r, c)]
    out = pl.pallas_call(
        functools.partial(assemble_kernel, stacked),
        in_specs=[pl.BlockSpec(memory_space=pltpu.SMEM)] + [pl.BlockSpec(memory_space=pltpu.VMEM)] * 8,
        out_specs=[pl.BlockSpec(memory_space=pltpu.VMEM)] * len(shapes),
        out_shape=[sds(shape, part.dtype) for shape in shapes],
        cost_estimate=cost(0, 4 * 32 * n * r * c),
        compiler_params=params(),
    )(me, *ins)
    if stacked:
        return token, [o.reshape(o.shape[0], 32 * r, c) for o in out]
    return token, out[0].reshape(32 * n * r, c)


def merge_kernel(counts, last, *refs):
    pairs_in = 2 * sum(counts)
    ins, outs = refs[:pairs_in], refs[pairs_in:]
    at = 0
    block = 0
    for half, count in enumerate(counts):
        mine = 0
        for _ in range(count):
            kept, got = ins[at], ins[at + 1]
            at += 2
            n, m = kept.shape[0], kept.shape[1]
            for j in range(n):
                v = (kept[j].astype(F32) + got[j].astype(F32)).astype(BF)
                if last:
                    outs[j][block : block + m] = v
                else:
                    outs[2 * half + (j >= n // 2)][j % (n // 2), mine : mine + m] = v
            mine += m
            block += m


def merge(parts, last):
    counts = [len(p) for p in parts]
    flat = [a for p in parts for pair in p for a in pair]
    n, _, r, c = flat[0].shape
    blocks = [sum(pair[0].shape[1] for pair in p) for p in parts]
    if last:
        shapes = [(sum(blocks), r, c)] * n
    else:
        shapes = [(n // 2, m, r, c) for m in blocks for _ in range(2)]
    return pl.pallas_call(
        functools.partial(merge_kernel, counts, last),
        in_specs=[pl.BlockSpec(memory_space=pltpu.VMEM)] * len(flat),
        out_specs=[pl.BlockSpec(memory_space=pltpu.VMEM)] * len(shapes),
        out_shape=[sds(shape, BF) for shape in shapes],
        cost_estimate=cost(0, 6 * n * sum(blocks) * r * c),
        compiler_params=params(),
    )(*flat)


class Reduction:
    def __init__(self, *halves):
        self.parts = [[(k, swap(s, CORE)) for k, s in half] for half in halves]
        self.stage = 0

    def step(self, *earlier):
        parts = self.parts
        if earlier:
            parts = after(parts, *earlier)
        if self.stage < 2:
            k0, s0, k1, s1 = merge(parts, False)
            self.parts = [[(k, swap(s, HALVES[i][1 - self.stage]))] for i, (k, s) in enumerate(((k0, s0), (k1, s1)))]
            self.token = (k0, k1)
        else:
            sums = merge(parts, True)
            self.terms = [sums[0]] + [swap(sums[k], k * Z) for k in range(1, 4)]
            self.token = (sums[0],)
        self.stage += 1
        return self


def prepare_kernel(hidden_ref, pooled_ref, low_ref, hidt_ref, lowt_ref, wide):
    hid = hidden_ref[0]
    half = pooled_ref.shape[1]
    hidt_ref[0] = hid.T
    columns = []
    for i in range(wide.shape[0]):
        wide[i] = hid[:, i * 128 : (i + 1) * 128].astype(F32)
        columns.append((wide[i, pl.ds(0, half, stride=2), :] + wide[i, pl.ds(1, half, stride=2), :]) * 0.5)
    pooled = jnp.concatenate(columns, axis=1)
    pooled_ref[0] = pooled
    low = pooled.astype(BF)
    low_ref[0] = low
    lowt_ref[0] = low.T


def prepare(hidden):
    B, L, D = hidden.shape
    R = L // 2
    return pl.pallas_call(
        prepare_kernel,
        grid=(B,),
        in_specs=[seqs(L, D)],
        out_specs=[seqs(R, D), seqs(R, D), seqs(D, L), seqs(D, R)],
        out_shape=[sds((B, R, D), F32), sds((B, R, D), BF), sds((B, D, L), BF), sds((B, D, R), BF)],
        scratch_shapes=[pltpu.VMEM((D // 128, L, 128), F32)],
        cost_estimate=cost(0, 8 * B * L * D),
        compiler_params=params(),
    )(hidden)


def attend_kernel(hidden_ref, pooled_ref, wq_ref, wk_ref, wv_ref, wr_ref, table_ref, small_ref, bias_ref,
                  ctx_ref, probs_ref, qu_ref, qw_ref, keys_ref, values_ref, rel_ref, rel_scr):
    half = hidden_ref.shape[1] // 2
    blk = half // 2

    @pl.when(pl.program_id(1) == 0)
    def _():
        rel = dot(table_ref[...], wr_ref[0]).astype(BF)
        rel_scr[...] = rel
        rel_ref[...] = rel

    hid = hidden_ref[0]
    q = dot(pooled_ref[0], wq_ref[0])
    qu = (q + small_ref[0:1, :]).astype(BF)
    qw = (q + small_ref[1:2, :]).astype(BF)
    qu_ref[0] = qu
    qw_ref[0] = qw
    keys_ref[0] = dot(hid, wk_ref[0]).astype(BF)
    values_ref[0] = (dot(hid, wv_ref[0]) + small_ref[2:3, :]).astype(BF)
    bias = bias_ref[0]
    lane = lax.broadcasted_iota(jnp.int32, (1, GC), 1)
    for b in range(2):
        rows = slice(b * blk, (b + 1) * blk)
        m0 = half * (1 - b)
        total = None
        for h in range(GH):
            mine = (lane >= h * HEAD) & (lane < (h + 1) * HEAD)
            quh = jnp.where(mine, qu[rows].astype(F32) * 0.125, 0.0).astype(BF)
            qwh = jnp.where(mine, qw[rows].astype(F32) * 0.125, 0.0).astype(BF)
            content = dot_nt(quh, keys_ref[0])
            placed = dot_nt(qwh, rel_scr[m0 : m0 + 3 * half, :])
            moved = pltpu.roll(placed, 0, 1, stride=2, stride_axis=0)[:, half:]
            s = content + moved + bias
            top = jnp.max(s, axis=-1, keepdims=True)
            e = jnp.exp(s - top)
            p = e * (1.0 / jnp.sum(e, axis=-1, keepdims=True))
            probs_ref[0, 0, h, rows, :] = p
            c = dot(p.astype(BF), values_ref[0])
            total = c if total is None else jnp.where(mine, c, total)
        ctx_ref[0, rows, :] = total.astype(BF)


def attend(hidden, pooled_low, weights_qk, weights_vr, table, small, bias):
    B, L, D = hidden.shape
    R = L // 2
    G = D // GC
    seq = lambda r: pl.BlockSpec((1, r, D), lambda g, s: (s, 0, 0))
    mat = lambda m: pl.BlockSpec((1, D, GC), lambda g, s: (m * G + g, 0, 0))
    so = lambda r: pl.BlockSpec((1, r, GC), lambda g, s: (s, 0, g))
    col = lambda r: pl.BlockSpec((r, GC), lambda g, s: (0, g))
    return pl.pallas_call(
        attend_kernel,
        grid=(G, B),
        in_specs=[seq(L), seq(R), mat(0), mat(1), mat(0), mat(1),
                  pl.BlockSpec((2 * L, D), lambda g, s: (0, 0)), col(small.shape[0]),
                  pl.BlockSpec((1, 1, L), lambda g, s: (s, 0, 0))],
        out_specs=[so(R), pl.BlockSpec((1, 1, GH, R, L), lambda g, s: (s, g, 0, 0, 0)),
                   so(R), so(R), so(L), so(L), col(2 * L)],
        out_shape=[sds((B, R, D), BF), sds((B, G, GH, R, L), F32), sds((B, R, D), BF), sds((B, R, D), BF),
                   sds((B, L, D), BF), sds((B, L, D), BF), sds((2 * L, D), BF)],
        scratch_shapes=[pltpu.VMEM((2 * L, GC), BF)],
        cost_estimate=cost(12e9, 60e6, B * G * GH * R * L),
        compiler_params=params(),
    )(hidden, pooled_low, weights_qk, weights_qk, weights_vr, weights_vr, table, small, bias[:, None, :])


def phi_and_slope(z):
    e = jnp.exp(z * z * (-0.5))
    t = 1.0 / (1.0 + (0.3275911 * 0.7071067811865476) * jnp.abs(z))
    poly = t * (0.127414796 + t * (-0.142248368 + t * (0.7107068705 + t * (-0.7265760135 + t * 0.5307027145))))
    tail = poly * e
    phi = jnp.where(z >= 0, 1.0 - tail, tail)
    return phi, phi + z * e * 0.3989422804014327


def norm(x):
    center = x - jnp.mean(x, axis=-1, keepdims=True)
    inv = lax.rsqrt(jnp.mean(center * center, axis=-1, keepdims=True) + EPSILON)
    return center * inv, inv


def norm_back(e, n, inv):
    return inv * (e - jnp.mean(e, axis=-1, keepdims=True) - n * jnp.mean(e * n, axis=-1, keepdims=True))


def add_rows(ref, *values):
    for k, v in enumerate(values):
        ref[k : k + 1, :] += jnp.sum(v, axis=0, keepdims=True)


def mlp_kernel(ctx_ref, pooled_ref, cot_ref, mask_ref, exp_ref, more_ref, w2_ref, small_ref, b1_ref,
               out_ref, y1_ref, n1_ref, s1_ref, inner_ref, slope_ref, dx2_ref, e2_ref, sums_ref):
    @pl.when(pl.program_id(0) == 0)
    def _():
        sums_ref[...] = jnp.zeros_like(sums_ref)

    row = lambda k: small_ref[k : k + 1, :]
    here = exp_ref.shape[0] - 1
    chunks = here + more_ref.shape[0]
    x1 = pooled_ref[0] + dot(ctx_ref[0], exp_ref[here]) + row(3)
    n1, inv1 = norm(x1)
    n1_ref[0] = n1
    s1_ref[0] = inv1
    y1 = n1 * row(4) + row(5)
    y1l = y1.astype(BF)
    y1_ref[0] = y1l
    x2 = y1 + row(6)
    for c in range(chunks):
        cs = slice(c * FC, (c + 1) * FC)
        z = dot(y1l, exp_ref[c] if c < here else more_ref[c - here]) + b1_ref[:, cs]
        phi, slope = phi_and_slope(z)
        inner = (z * phi).astype(BF)
        inner_ref[0, :, cs] = inner
        slope_ref[0, :, cs] = slope
        x2 += dot(inner, w2_ref[cs, :])
    n2, inv2 = norm(x2)
    m = mask_ref[0]
    out_ref[0] = ((n2 * row(7) + row(8)) * m).astype(BF)
    dy2 = cot_ref[0].astype(F32) * m
    dx2 = norm_back(dy2 * row(7), n2, inv2)
    dx2_ref[0] = dx2
    e2_ref[0] = dx2.astype(BF)
    add_rows(sums_ref, dx2, dy2 * n2, dy2)


def mlp(ctx, pooled, cot, mask, expand, more, w2, small, b1):
    B, R, D = pooled.shape
    F = w2.shape[0]
    return pl.pallas_call(
        mlp_kernel,
        grid=(B,),
        in_specs=[seqs(R, D), seqs(R, D), seqs(R, D), seqs(R, 1), whole(*expand.shape), whole(*more.shape), whole(F, D),
                  whole(*small.shape), whole(1, F)],
        out_specs=[seqs(R, D), seqs(R, D), seqs(R, D), seqs(R, 1), seqs(R, F), seqs(R, F), seqs(R, D), seqs(R, D),
                   pl.BlockSpec((8, D), lambda s: (0, 0))],
        out_shape=[sds((B, R, D), BF), sds((B, R, D), BF), sds((B, R, D), F32), sds((B, R, 1), F32), sds((B, R, F), BF),
                   sds((B, R, F), F32), sds((B, R, D), F32), sds((B, R, D), BF), sds((8, D), F32)],
        cost_estimate=cost(10e9, 40e6, 2 * B * R * F),
        compiler_params=params(),
    )(ctx, pooled, cot, mask, expand, more, w2, small, b1)


def mlp_back_kernel(dx2_ref, e2_ref, slope_ref, n1_ref, s1_ref, exp_ref, more_ref, w2_ref, small_ref,
                    e1_ref, dx1_ref, ea_ref, dctx_ref, sums_ref, db1_ref):
    @pl.when(pl.program_id(0) == 0)
    def _():
        sums_ref[...] = jnp.zeros_like(sums_ref)
        db1_ref[...] = jnp.zeros_like(db1_ref)

    here = exp_ref.shape[0] - 1
    chunks = here + more_ref.shape[0]
    e2 = e2_ref[0]
    dy1 = dx2_ref[0]
    for c in range(chunks):
        cs = slice(c * FC, (c + 1) * FC)
        dz = dot_nt(e2, w2_ref[cs, :]) * slope_ref[0, :, cs]
        db1_ref[:, cs] += jnp.sum(dz, axis=0, keepdims=True)
        e1 = dz.astype(BF)
        e1_ref[0, :, cs] = e1
        dy1 += dot_nt(e1, exp_ref[c] if c < here else more_ref[c - here])
    n1 = n1_ref[0]
    dx1 = norm_back(dy1 * small_ref[4:5, :], n1, s1_ref[0])
    dx1_ref[0] = dx1
    ea = dx1.astype(BF)
    ea_ref[0] = ea
    dctx_ref[0] = dot_nt(ea, exp_ref[here]).astype(BF)
    add_rows(sums_ref, dx1, dy1 * n1, dy1)


def mlp_back(dx2, e2, slope, n1, s1, expand, more, w2, small):
    B, R, D = dx2.shape
    F = w2.shape[0]
    return pl.pallas_call(
        mlp_back_kernel,
        grid=(B,),
        in_specs=[seqs(R, D), seqs(R, D), seqs(R, F), seqs(R, D), seqs(R, 1), whole(*expand.shape), whole(*more.shape), whole(F, D),
                  whole(*small.shape)],
        out_specs=[seqs(R, F), seqs(R, D), seqs(R, D), seqs(R, D), pl.BlockSpec((8, D), lambda s: (0, 0)),
                   pl.BlockSpec((1, F), lambda s: (0, 0))],
        out_shape=[sds((B, R, F), BF), sds((B, R, D), F32), sds((B, R, D), BF), sds((B, R, D), BF), sds((8, D), F32),
                   sds((1, F), F32)],
        cost_estimate=cost(7e9, 50e6),
        compiler_params=params(),
    )(dx2, e2, slope, n1, s1, expand, more, w2, small)


def deal(half, me, total_ref, put):
    r = total_ref.shape[0] // 32
    for rel in range(32):
        k = jnp.bitwise_xor(me, flat_of(rel, half))
        put(rel // 16, rel % 16, total_ref[pl.ds(pl.multiple_of(k * r, 8), r), :].astype(BF))


def outer_kernel(half, me_ref, a_ref, b_ref, keep_ref, send_ref, turned, total):
    B, R, M = a_ref.shape

    @pl.when(pl.program_id(0) == 0)
    def _():
        turned[...] = a_ref[...].reshape(B * R, M).T

    total[...] = dot(turned[...], b_ref[...].reshape(B * R, b_ref.shape[2]))

    def put(sent, i, v):
        (send_ref if sent else keep_ref)[i, 0] = v

    deal(half, me_ref[0], total, put)


def outer_plain_kernel(a_ref, b_ref, out_ref):
    B, R, M = a_ref.shape
    out_ref[...] = dot_tn(a_ref[...].reshape(B * R, M), b_ref[...].reshape(B * R, b_ref.shape[2]))


def outer(me, a, b, cols, half=None, blocks=None):
    B, R, M = a.shape
    N = b.shape[2]
    first, count = blocks or (0, N // cols)
    specs = [pl.BlockSpec((B, R, M), lambda j: (0, 0, 0)), pl.BlockSpec((B, R, cols), lambda j: (0, 0, first + j))]
    price = cost(1.5 * B * R * M * cols * count, 2 * (B * R * (M + cols * count) + M * cols * count))
    if half is None:
        return pl.pallas_call(
            outer_plain_kernel, grid=(count,), in_specs=specs,
            out_specs=pl.BlockSpec((M, cols), lambda j: (0, j)),
            out_shape=sds((M, N), F32), cost_estimate=price, compiler_params=params())(a, b)
    return pl.pallas_call(
        functools.partial(outer_kernel, half),
        grid=(count,),
        in_specs=[pl.BlockSpec(memory_space=pltpu.SMEM)] + specs,
        out_specs=[pl.BlockSpec((16, 1, M // 32, cols), lambda j: (0, j, 0, 0))] * 2,
        out_shape=[sds((16, count, M // 32, cols), BF)] * 2,
        scratch_shapes=[pltpu.VMEM((M, B * R), BF), pltpu.VMEM((M, cols), F32)],
        cost_estimate=price,
        compiler_params=params(),
    )(me, a, b)


def tall_outer_kernel(steps, me_ref, a_ref, b_ref, keep0_ref, send0_ref, keep1_ref, send1_ref, total):
    B, R, M = a_ref.shape
    i = pl.program_id(0)
    v = dot_tn(a_ref[...].reshape(B * R, M), b_ref[...].reshape(B * R, b_ref.shape[2]))
    total[pl.ds(pl.multiple_of(i * M, 8), M), :] = v

    @pl.when(i == steps - 1)
    def _():
        r = keep0_ref.shape[2]
        for half, refs in enumerate(((keep0_ref, send0_ref), (keep1_ref, send1_ref))):
            for rel in range(32):
                k = jnp.bitwise_xor(me_ref[0], flat_of(rel, half))
                at = pl.multiple_of(k * (2 * r) + half * r, 8)
                refs[rel // 16][rel % 16, 0] = total[pl.ds(at, r), :].astype(BF)


def tall_outer(me, a, b, rows):
    B, R, M = a.shape
    N = b.shape[2]
    r = M // 64
    out = pl.pallas_call(
        functools.partial(tall_outer_kernel, M // rows),
        grid=(M // rows,),
        in_specs=[pl.BlockSpec(memory_space=pltpu.SMEM), pl.BlockSpec((B, R, rows), lambda i: (0, 0, i)), whole(B, R, N)],
        out_specs=[whole(16, 1, r, N)] * 4,
        out_shape=[sds((16, 1, r, N), BF)] * 4,
        scratch_shapes=[pltpu.VMEM((M, N), F32)],
        cost_estimate=cost(1.5 * B * R * M * N, 2 * (B * R * (M + N) + M * N)),
        compiler_params=params(),
    )(me, a, b)
    return (out[0], out[1]), (out[2], out[3])


def small_deal_kernel(me_ref, *refs):
    sums, (sums1, sums2, db1, keep_ref, send_ref, total, turned) = refs[:-7], refs[-7:]
    D = sums1.shape[1]
    total[...] = jnp.zeros_like(total)
    for g, s in enumerate(sums):
        total[0:3, g * GC : (g + 1) * GC] = s[0:3, :]
    total[3:6, :] = sums1[0:3, :]
    total[6:9, :] = sums2[0:3, :]
    for i in range(db1.shape[1] // D):
        total[9 + i : 10 + i, :] = db1[0:1, i * D : (i + 1) * D]
    turned[...] = jnp.concatenate([total[...].T, jnp.zeros((D, GC - total.shape[0]), F32)], axis=1)

    def put(sent, i, v):
        (send_ref if sent else keep_ref)[i, 0] = v

    deal(0, me_ref[0], turned, put)


def small_deal(me, sums, sums1, sums2, db1):
    D = sums1.shape[1]
    n = 4 + len(sums)
    return pl.pallas_call(
        small_deal_kernel,
        in_specs=[pl.BlockSpec(memory_space=pltpu.SMEM)] + [pl.BlockSpec(memory_space=pltpu.VMEM)] * (n - 1),
        out_specs=[pl.BlockSpec(memory_space=pltpu.VMEM)] * 2,
        out_shape=[sds((16, 1, D // 32, GC), BF)] * 2,
        scratch_shapes=[pltpu.VMEM((128, D), F32), pltpu.VMEM((D, GC), F32)],
        cost_estimate=cost(0, 4e6),
        compiler_params=params(),
    )(me, *sums, sums1, sums2, db1)


def attend_back_kernel(plan, *refs):
    (me_ref, probs_ref, dctx_ref, qu_ref, qw_ref, keys_ref, values_ref, rel_ref, hidt_ref, lowt_ref, tablet_ref) = refs[:11]
    outs = refs[11 : 14]
    dq_ref, dk_ref, dv_ref = outs
    grads = refs[14 : -8]
    sums_ref = refs[-8]
    acc_q, acc_k, acc_v, acc_r, acc_dv, dkt, dvt = refs[-7:]
    step = pl.program_id(0)
    half, L = probs_ref.shape[3], probs_ref.shape[4]
    blk = half // 2

    @pl.when(step == 0)
    def _():
        for a in (acc_q, acc_k, acc_v, acc_r, acc_dv, sums_ref):
            a[...] = jnp.zeros_like(a)

    across = lax.broadcasted_iota(jnp.int32, (half, half), 0) + lax.broadcasted_iota(jnp.int32, (half, half), 1)
    flip = (across == half - 1).astype(F32).astype(BF)
    lane = lax.broadcasted_iota(jnp.int32, (1, GC), 1)
    dctx = dctx_ref[0]
    dctx_t = dctx.T
    qu_t = qu_ref[0].T
    qwr_t = dot(flip, qw_ref[0]).astype(BF).T
    keys = keys_ref[0]
    values = values_ref[0]
    dqu = dqw = None
    for h in range(GH):
        mine = (lane >= h * HEAD) & (lane < (h + 1) * HEAD)
        sel = slice(h * HEAD, (h + 1) * HEAD)
        p = probs_ref[0, 0, h]
        dp = dot_nt(jnp.where(mine, dctx.astype(F32), 0.0).astype(BF), values)
        t = p * dp
        draw = (t - p * jnp.sum(t, axis=-1, keepdims=True)).astype(BF)
        dvt[sel, :] = dot(dctx_t[sel], p.astype(BF))
        both = dot(jnp.concatenate([qu_t[sel], flip], axis=0), draw)
        dkt[sel, :] = both[:HEAD] * 0.125
        back = both[HEAD:]
        a = dot(back.astype(BF), keys)
        tables = []
        for b in range(2):
            x = jnp.concatenate([back[b * blk : (b + 1) * blk], jnp.zeros((blk, half), F32)], axis=1)
            x = pltpu.roll(x, 2, 1, stride=2, stride_axis=0).astype(BF)
            m0 = half * b
            tables.append(dot(x, rel_ref[m0 : m0 + 3 * half, :]))
            acc_r[sel, m0 : m0 + 3 * half] += dot(qwr_t[sel, b * blk : (b + 1) * blk], x)
        c = jnp.concatenate(tables, axis=0)
        dqu, dqw = (a, c) if dqu is None else (jnp.where(mine, a, dqu), jnp.where(mine, c, dqw))
    dqu = dqu * 0.125
    dqw = dqw * 0.125
    dq = dot(flip, (dqu + dqw).astype(BF)).astype(BF)
    dk = dkt[...].astype(BF).T
    dvf = dvt[...]
    dv = dvf.astype(BF).T
    dq_ref[0] = dq
    dk_ref[0] = dk
    dv_ref[0] = dv
    acc_dv[...] += dvf
    add_rows(sums_ref, dqu, dqw)
    acc_q[...] += dot(lowt_ref[0], dq)
    acc_k[...] += dot(hidt_ref[0], dk)
    acc_v[...] += dot(hidt_ref[0], dv)

    @pl.when(step == pl.num_programs(0) - 1)
    def _():
        sums_ref[2:3, :] = jnp.sum(acc_dv[...].T, axis=0, keepdims=True)
        dr = acc_r[...] * 0.125
        hi = dr.astype(BF)
        lo = (dr - hi.astype(F32)).astype(BF)
        tt = tablet_ref[...]
        if plan is None:
            for i, a in enumerate((acc_q, acc_k, acc_v)):
                grads[0][i] = a[...]
            grads[0][3] = dot_nt(tt, hi) + dot_nt(tt, lo)
        else:
            for i in range(4):
                half = plan[i]
                at = plan[:i].count(half)
                base = 2 * sorted(set(plan)).index(half)
                acc = (acc_q, acc_k, acc_v, acc_q)[i]
                if i == 3:
                    acc_q[...] = dot_nt(tt, hi) + dot_nt(tt, lo)

                def put(sent, j, v):
                    grads[base + sent][j, at] = v

                deal(half, me_ref[0], acc, put)


def attend_back(me, g, probs, dctx, qu, qw, keys, values, rel, hid_t, low_t, table_t, plan=None):
    B, R, D = qu.shape
    L = 2 * R
    so = lambda r: pl.BlockSpec((1, r, GC), lambda s: (s, 0, g))
    if plan is None:
        grad_specs = [pl.BlockSpec((4, D, GC), lambda s: (0, 0, 0))]
        grad_shapes = [sds((4, D, GC), F32)]
    else:
        sizes = [(16, plan.count(h), D // 32, GC) for h in sorted(set(plan)) for _ in range(2)]
        grad_specs = [whole(*size) for size in sizes]
        grad_shapes = [sds(size, BF) for size in sizes]
    return pl.pallas_call(
        functools.partial(attend_back_kernel, plan),
        grid=(B,),
        in_specs=[pl.BlockSpec(memory_space=pltpu.SMEM),
                  pl.BlockSpec((1, 1, GH, R, L), lambda s: (s, g, 0, 0, 0)), so(R), so(R), so(R), so(L), so(L),
                  pl.BlockSpec((2 * L, GC), lambda s: (0, g)), seqs(D, L), seqs(D, R), whole(D, 2 * L)],
        out_specs=[seqs(R, GC), seqs(L, GC), seqs(L, GC)] + grad_specs + [pl.BlockSpec((8, GC), lambda s: (0, 0))],
        out_shape=[sds((B, R, GC), BF), sds((B, L, GC), BF), sds((B, L, GC), BF)] + grad_shapes + [sds((8, GC), F32)],
        scratch_shapes=[pltpu.VMEM((D, GC), F32)] * 3 + [pltpu.VMEM((GC, 2 * L), F32)] + [pltpu.VMEM((GC, L), F32)] * 3,
        cost_estimate=cost(10e9, 30e6),
        compiler_params=params(),
    )(me, probs, dctx, qu, qw, keys, values, rel, hid_t, low_t, table_t)


def input_grad_kernel(groups, *refs):
    dqs, dks, dvs = refs[:groups], refs[groups : 2 * groups], refs[2 * groups : 3 * groups]
    dx1_ref, wa_ref, wb_ref, out_ref, wide = refs[3 * groups :]
    half = dx1_ref.shape[1]
    shared = dx1_ref[0]
    total = None
    for g in range(groups):
        shared += dot_nt(dqs[g][0], wa_ref[g])
        t = dot_nt(dks[g][0], wa_ref[groups + g]) + dot_nt(dvs[g][0], wb_ref[g])
        total = t if total is None else total + t
    shared = shared * 0.5
    for i in range(wide.shape[0]):
        cs = slice(i * 128, (i + 1) * 128)
        wide[i, pl.ds(0, half, stride=2), :] = shared[:, cs]
        wide[i, pl.ds(1, half, stride=2), :] = shared[:, cs]
        out_ref[0, :, cs] = (total[:, cs] + wide[i]).astype(BF)


def input_grad(dqs, dks, dvs, dx1, weights_qk, weights_vr):
    B, R, D = dx1.shape
    L = 2 * R
    G = len(dqs)
    return pl.pallas_call(
        functools.partial(input_grad_kernel, G),
        grid=(B,),
        in_specs=[seqs(R, GC)] * G + [seqs(L, GC)] * (2 * G) + [seqs(R, D), whole(2 * G, D, GC), whole(G, D, GC)],
        out_specs=seqs(L, D),
        out_shape=sds((B, L, D), BF),
        scratch_shapes=[pltpu.VMEM((D // 128, L, 128), F32)],
        cost_estimate=cost(5e9, 20e6),
        compiler_params=params(),
    )(*dqs, *dks, *dvs, dx1, weights_qk, weights_vr)


def adamw(weight, moment, second, gradient, rates):
    new_moment = rates[1] * moment + (1.0 - rates[1]) * gradient
    new_second = rates[2] * second + (1.0 - rates[2]) * gradient * gradient
    moment_hat = new_moment / rates[4]
    second_hat = new_second / rates[5]
    new_weight = weight - rates[0] * (moment_hat / (jnp.sqrt(second_hat) + 1e-08) + rates[3] * weight)
    return (new_weight, new_moment, new_second)


def update_kernel(plan, rates_ref, w_ref, m_ref, v_ref, *refs):
    terms, (grad_ref, w_out, m_out, v_out) = refs[:-4], refs[-4:]
    rates = [rates_ref[i] for i in range(6)]
    for first, count, block, dest in plan:
        g = None
        for t in terms[first : first + count]:
            v = (t[...] if block is None else t[block]).astype(F32)
            g = v if g is None else g + v
        grad_ref[dest] = g
        w_out[dest], m_out[dest], v_out[dest] = adamw(w_ref[dest], m_ref[dest], v_ref[dest], g, rates)


def update(rates, w, m, v, terms, plan=None):
    plan = plan or [(0, len(terms), None, (slice(None),) * w.ndim)]
    return pl.pallas_call(
        functools.partial(update_kernel, plan),
        in_specs=[pl.BlockSpec(memory_space=pltpu.SMEM)] + [pl.BlockSpec(memory_space=pltpu.VMEM)] * (3 + len(terms)),
        out_specs=[pl.BlockSpec(memory_space=pltpu.VMEM)] * 4,
        out_shape=[sds(w.shape, F32)] * 4,
        cost_estimate=cost(0, 36 * w.size),
        compiler_params=params(),
    )(rates, w, m, v, *terms)


def shards(fast, hidden, lengths, key_mask, cotangent, attention_weight, expand_weight, contract_weight, small_params,
           mean_attention, mean_expand, mean_contract, mean_small,
           square_attention, square_expand, square_contract, square_small, update_step, update_rates):
    B, L, D = hidden.shape
    R = L // 2
    F = expand_weight.shape[1]
    G = D // GC
    C = F // FC
    H = C // 2
    r = attention_weight.shape[1]
    V = small_params.shape[0]
    me = (lax.axis_index("dp") * lax.axis_size("fsdp") + lax.axis_index("fsdp")).astype(jnp.int32).reshape(1)

    cut = lambda a, c: a.astype(BF).reshape(r, -1, c).transpose(1, 0, 2)
    small_t = jnp.pad(small_params.T, ((0, 0), (0, GC - V))).astype(BF)[None]
    a_low = attention_weight
    first = jnp.concatenate([cut(a_low[0], GC), cut(a_low[1], GC), small_t, cut(a_low[2], GC), cut(a_low[3], GC)], axis=0)
    e_cut = cut(expand_weight, FC)
    second = jnp.concatenate([e_cut[:H], cut(a_low[4], FC), e_cut[H:]], axis=0)
    if fast:
        token, (w_qk, w_vr) = gather(me, first, 2 * G + 1)
        token, (w_eo, w_e) = gather(me, after(second, token), H + 1)
        third = contract_weight.astype(BF).reshape(2, -1, D)
        token, w2 = gather(me, after(third, token), 1, stacked=False)
    else:
        full = lambda a: lax.all_gather(a, ALL, axis=1, tiled=True)
        first, second = full(first), full(second)
        w_qk, w_vr = first[: 2 * G + 1], first[2 * G + 1 :]
        w_eo, w_e = second[: H + 1], second[H + 1 :]
        w2 = lax.all_gather(contract_weight.astype(BF), ALL, axis=0, tiled=True)
    small = w_qk[2 * G, :, :16].astype(F32).T
    b1 = small[9:V].reshape(1, F)

    positions = jnp.arange(L, dtype=jnp.int32)
    valid = (key_mask == 1) & (positions[None, :] < lengths[:, None])
    bias = jnp.where(valid, 0.0, MASK_FILL).astype(F32)
    mask = jnp.max(valid.astype(F32).reshape(B, R, 2), axis=2)[:, :, None]
    table = rel_table(L, D).astype(BF)
    table_t = table.T
    step = update_step[0].astype(F32)
    rates = jnp.concatenate([update_rates, 1.0 - jnp.power(update_rates[1:3], step)])

    pooled, pooled_low, hid_t, low_t = prepare(hidden)
    ctx, probs, qu, qw, keys, values, rel = attend(hidden, pooled_low, w_qk, w_vr, table, small, bias)
    out, y1, n1, s1, inner, slope, dx2, e2, sums2 = mlp(ctx, pooled, cotangent, mask, w_eo, w_e, w2, small, b1)

    def backward(g, dctx, plan=None):
        return attend_back(me, g, probs, dctx, qu, qw, keys, values, rel, hid_t, low_t, table_t, plan)

    if not fast:
        scatter = lambda a, d: lax.psum_scatter(a, ALL, scatter_dimension=d, tiled=True)
        e1, dx1, ea, dctx, sums1, db1 = mlp_back(dx2, e2, slope, n1, s1, w_eo, w_e, w2, small)
        back = [backward(g, dctx) for g in range(G)]
        in_grad = input_grad([b[0] for b in back], [b[1] for b in back], [b[2] for b in back], dx1, w_qk, w_vr)
        d_att = jnp.concatenate([b[3] for b in back], axis=2)
        d_att = jnp.concatenate([d_att, outer(me, ctx, ea, 384)[None]], axis=0)
        d_small = jnp.concatenate([b[-1][0:3] for b in back], axis=1)
        d_small = jnp.concatenate([d_small, sums1[0:3], sums2[0:3], db1.reshape(-1, D)], axis=0)
        attention_terms, attention_plan = [scatter(d_att, 1)], None
        expand_terms, expand_plan = [scatter(outer(me, y1, e1, FC), 0)], None
        contract_terms, contract_plan = [scatter(outer(me, inner, e2, 384), 0)], None
        small_grad = scatter(d_small, 1)
    else:
        half0, half1 = tall_outer(me, inner, e2, 768)
        red1 = Reduction([half0], [half1])
        e1, dx1, ea, dctx, sums1, db1 = mlp_back(dx2, after(e2, half0, half1), slope, n1, s1, w_eo, w_e, w2, small)
        red1.step(e1)
        y1, ctx = after((y1, ctx), red1.token)
        d_e0 = outer(me, y1, e1, FC, 0, (0, H))
        d_e1 = outer(me, y1, e1, FC, 1, (H, C - H))
        d_o = outer(me, ctx, ea, FC, 0)
        red2 = Reduction([d_e0, d_o], [d_e1])
        back = [backward(0, after(dctx, d_e0, d_e1, d_o), (0, 0, 0, 0))]
        red1.step(back[0][0])
        red2.step(back[0][0])
        back.append(backward(1, after(dctx, red1.token, red2.token), (1, 1, 1, 1)))
        red3 = Reduction([tuple(back[0][3:5])], [tuple(back[1][3:5])])
        red1.step(back[1][0])
        red2.step(back[1][0])
        back.append(backward(2, after(dctx, red1.token, red2.token), (0, 0, 1, 1)))
        last = back[2]
        d_small = small_deal(me, [b[-1] for b in back], sums1, sums2, db1)
        red4 = Reduction([tuple(last[3:5]), tuple(d_small)], [tuple(last[5:7])])
        red2.step(last[0])
        red3.step(last[0])
        red4.step()
        dx1 = after(dx1, red2.token, red3.token, red4.token)
        in_grad = input_grad([b[0] for b in back], [b[1] for b in back], [b[2] for b in back], dx1, w_qk, w_vr)
        red3.step(in_grad)
        red4.step(in_grad)
        red3.step()
        red4.step()
        whole_rows = slice(None)
        r2 = contract_weight.shape[0] // 2
        contract_terms = red1.terms
        contract_plan = [(0, 4, i, (slice(i * r2, (i + 1) * r2), whole_rows)) for i in range(2)]
        expand_terms = red2.terms
        expand_plan = [(0, 4, i + (i >= H), (whole_rows, slice(i * FC, (i + 1) * FC))) for i in range(C)]
        attention_terms = red3.terms + red4.terms + red2.terms
        place = lambda m, g: (m, whole_rows, slice(g * GC, (g + 1) * GC))
        attention_plan = [(0, 4, 4 * g + m, place(m, g)) for g in range(2) for m in range(4)]
        attention_plan += [(4, 4, m + (m > 1), place(m, 2)) for m in range(4)]
        attention_plan += [(8, 4, H, (4, whole_rows, whole_rows))]
        small_grad = sum(t[2, :, :V].astype(F32) for t in red4.terms).T
    contract_up = update(rates, contract_weight, mean_contract, square_contract, contract_terms, contract_plan)
    expand_up = update(rates, expand_weight, mean_expand, square_expand, expand_terms, expand_plan)
    attention_up = update(rates, attention_weight, mean_attention, square_attention, attention_terms, attention_plan)
    small_up = update(rates, small_params, mean_small, square_small, [small_grad])
    ups = (attention_up, expand_up, contract_up, small_up)
    return (out, in_grad) + tuple(u[i] for i in range(4) for u in ups)


def solution(mesh):
    outer_rows = P(ALL, None)
    middle = P(None, ALL, None)
    inner_cols = P(None, ALL)
    table = (middle, outer_rows, outer_rows, inner_cols)
    tokens = P(ALL, None, None)
    in_specs = (tokens, P(ALL), outer_rows, tokens) + table * 3 + (P(), P())
    out_specs = (tokens, tokens) + table * 4
    fast = mesh.shape["dp"] == 8 and mesh.shape["fsdp"] == 4
    return jax.shard_map(
        functools.partial(shards, fast), mesh=mesh, in_specs=in_specs, out_specs=out_specs, check_vma=False
    )
```

time: 1670 us -> 488 us (0.29)
  other arithmetic: 635 us -> 12.5 us
  local copies, waits for them, and re-layouts: 421 us -> 30.6 us
  Pallas kernels: 0 us -> 289 us
  matrix products: 263 us -> 0 us
  waiting for transfers between devices: 190 us -> 72.5 us
  blocking collectives: 113 us -> 0 us
  starting transfers between devices: 0.37 us -> 70.9 us
    select_n x85 -> x1, other arithmetic: 544 us -> 0.01 us  [shards(): bias = jnp.where(valid, 0.0, MASK_FILL).astype(F32)]
    pallas_call x0 -> x32, Pallas kernels: none -> 289 us  [the longest x3 69.6 us: attend_back(): pl.pallas_call(functools.partial(attend_back_kernel, plan), grid=(B,), in...]
    slice x64 -> x4, local copies, waits for them, and re-layouts: 276 us -> 0.34 us  [the longest x2 0.31 us: shards(): b1 = small[9:V].reshape(1, F)]
    dot_general x60 -> x0, matrix products: 236 us -> none  [the longest x4 16.7 us: attend_back(): jnp.einsum('phe,she->hps', content_heads, keys_heads, preferred_element_t...]
    all_gather x6 -> x0, waiting for transfers between devices: 137 us -> none  [the longest x2 50.7 us: collect(): lax.all_gather(expand_part, ('dp', 'fsdp'), axis=0, tiled=True)]
    ppermute x0 -> x71, waiting for transfers between devices: none -> 72.5 us  [swap(): return lax.ppermute(a, ALL, pairs(bit))]
    all_gather x1 -> x0, blocking collectives: 71.2 us -> none  [collect(): lax.all_gather(small_part, ('dp', 'fsdp'), axis=1, tiled=True)]
    ppermute x0 -> x71, starting transfers between devices: none -> 70.9 us  [swap(): return lax.ppermute(a, ALL, pairs(bit))]
  transfers between devices with their start and end apart: 9 -> 71, of which waited for: 4 -> 14; matrix products, arithmetic and copies ran while one was open for 74% -> 7% of each run, Pallas kernels for 0% -> 45%
where the time goes in v1:
time: 488 us; the launch traced here: 478 us
  Pallas kernels  289 us (59%)
  waiting for transfers between devices  72.5 us (15%)
  starting transfers between devices  70.9 us (15%)
  local copies, waits for them, and re-layouts  30.6 us (6%)
  other arithmetic  12.5 us (3%)
    ppermute x71, waiting for transfers between devices, swap(): return lax.ppermute(a, ALL, pairs(bit))  72.5 us
    ppermute x71, starting transfers between devices, swap(): return lax.ppermute(a, ALL, pairs(bit))  70.9 us
    pallas_call x3, Pallas kernels, attend_back(): pl.pallas_call(functools.partial(attend_back_kernel, plan), grid=(B,), in...  69.6 us
    pallas_call x1, Pallas kernels, attend(): pl.pallas_call(attend_kernel, grid=(G, B), in_specs=[seq(L), seq(R), mat(...  62.4 us
    pallas_call x12, Pallas kernels, merge(): pl.pallas_call(functools.partial(merge_kernel, counts, last), in_specs=[p...  32.3 us
    pallas_call x1, Pallas kernels, mlp(): pl.pallas_call(mlp_kernel, grid=(B,), in_specs=[seqs(R, D), seqs(R, D), s...  30.6 us
    pallas_call x1, Pallas kernels, mlp_back(): pl.pallas_call(mlp_back_kernel, grid=(B,), in_specs=[seqs(R, D), seqs(R,...  20.9 us
    pallas_call x3, Pallas kernels, outer(): pl.pallas_call(functools.partial(outer_kernel, half), grid=(count,), in_s...  17.7 us
  transfers between devices with their start and end apart: 71, of which 14 were waited for; matrix products, arithmetic and copies ran while one was open for 7% of the time, Pallas kernels for 45%

profile of v1, /device:TPU:0, one launch (start us, length us, event | category | flops | bytes accessed | tf_op | source)
XLA Modules:
  0.0 478.4 jit_solution(1539981327555251194)
XLA Ops:
  2.7 5.1 %collective-permute-start.2 = (bf16[13,24,256]{2,1,0:T(8,128)(2,1)S(1)}, bf16[13,24,256]{2,1,0:T(8,128)(2,1)S(1)}, u32[]{:S(2)}, u32[]{:S(2)}) collective-permute-start(bf16[13,24,256]{2,1,0:T(8,128)(2,1)S(1)} %get-tuple-element.366), channel_id=1, source_target_pairs={{0,24},{1,25},{2,26},{3,27},{4,28},{5,29},{6,30},{7,31},{8,16},{9,... | collective-permute-start | bytes 479240 | tf_op jit(solution)/shard_map/ppermute | solution.py:74
  8.7 6.0 %fusion = (bf16[1024,384]{0,1:T(8,128)(2,1)S(1)}, bf16[1024,384]{0,1:T(8,128)(2,1)S(1)}) fusion(f32[384]{0:T(512)S(1)} %multiply_exponential_fusion, f32[1024]{0:T(1024)S(1)} %iota_subtract_fusion), kind=kLoop, calls=%fused_computation.2 | loop fusion | flops 1179648 | bytes 1578496 | tf_op jit(solution)/shard_map/convert.4
  14.8 6.6 %collective-permute-done.1 = bf16[13,24,256]{2,1,0:T(8,128)(2,1)S(1)} collective-permute-done((bf16[13,24,256]{2,1,0:T(8,128)(2,1)S(1)}, bf16[13,24,256]{2,1,0:T(8,128)(2,1)S(1)}, u32[]{:S(2)}, u32[]{:S(2)}) %collective-permute-start.1) | collective-permute-done | bytes 159776 | tf_op jit(solution)/shard_map/ppermute | solution.py:74
  31.0 7.0 %collective-permute-done.12 = bf16[5,24,768]{2,1,0:T(8,128)(2,1)S(1)} collective-permute-done((bf16[5,24,768]{2,1,0:T(8,128)(2,1)S(1)}, bf16[5,24,768]{2,1,0:T(8,128)(2,1)S(1)}, u32[]{:S(2)}, u32[]{:S(2)}) %collective-permute-start.12) | collective-permute-done | bytes 184352 | tf_op jit(solution)/shard_map/ppermute | solution.py:74
  48.4 3.6 collective-permute-done.23
  59.9 4.3 collective-permute-done.29
  65.6 13.1 %collective-permute-done.4.refs_1_ = bf16[8,7,24,256]{3,2,1,0:T(8,128)(2,1)} collective-permute-done((bf16[8,7,24,256]{3,2,1,0:T(8,128)(2,1)S(1)}, bf16[8,7,24,256]{3,2,1,0:T(8,128)(2,1)}, u32[]{:S(2)}, u32[]{:S(2)}) %collective-permute-start.4) | collective-permute-done | bytes 688160 | tf_op jit(solution)/shard_map/ppermute | solution.py:74
  84.8 6.2 %shard_map.313 = (f32[4,256,768]{2,1,0:T(8,128)}, bf16[4,256,768]{2,1,0:T(8,128)(2,1)}, bf16[4,768,512]{2,1,0:T(8,128)(2,1)}, bf16[4,768,256]{2,1,0:T(8,128)(2,1)}) custom-call(bf16[4,512,768]{2,1,0:T(8,128)(2,1)} %hidden_ref.3), custom_call_target="tpu_custom_call" | custom-call | bytes 12582912 | tf_op jit(solution)/shard_map/pallas_call | solution.py:203
  95.9 12.3 %collective-permute-done.30.refs_5_ = bf16[8,1,48,768]{3,2,1,0:T(8,128)(2,1)} collective-permute-done((bf16[8,1,48,768]{3,2,1,0:T(8,128)(2,1)}, bf16[8,1,48,768]{3,2,1,0:T(8,128)(2,1)}, u32[]{:S(2)}, u32[]{:S(2)}) %collective-permute-start.30) | collective-permute-done | bytes 589856 | tf_op jit(solution)/shard_map/ppermute | solution.py:74
  114.1 5.2 %shard_map.314 = (bf16[7,32,24,256]{3,2,1,0:T(8,128)(2,1)}, bf16[6,32,24,256]{3,2,1,0:T(8,128)(2,1)}) custom-call(s32[1]{0:T(128)} %bitcast.me_ref.refs_0_, bf16[8,7,24,256]{3,2,1,0:T(8,128)(2,1)} %copy-done.9, bf16[8,7,24,256]{3,2,1,0:T(8,128)(2,1)} %collective-permute-done.4.refs_1_, bf16[8,7,24,256]{3,2,1,0:T(8,128)(2,1)} %copy-done.17, ...), custom_call_target="tpu_custom_call" | custom-call | bytes 10223616 | tf_op jit(solution)/shard_map/pallas_call | solution.py:111
  124.4 62.4 %shard_map.315 = (bf16[4,256,768]{2,1,0:T(8,128)(2,1)}, f32[4,3,4,256,512]{4,3,2,1,0:T(8,128)}, bf16[4,256,768]{2,1,0:T(8,128)(2,1)}, bf16[4,256,768]{2,1,0:T(8,...) custom-call(bf16[4,512,768]{2,1,0:T(8,128)(2,1)} %hidden_ref.3, ...), custom_call_target="tpu_custom_call" | custom-call | flops 24000000000 | bytes 60000000 | tf_op jit(solution)/shard_map/pallas_call | solution.py:265
  187.8 4.7 shard_map.317
  192.6 5.8 %shard_map.316 = (bf16[3,32,24,768]{3,2,1,0:T(8,128)(2,1)}, bf16[2,32,24,768]{3,2,1,0:T(8,128)(2,1)}) custom-call(s32[1]{0:T(128)} %bitcast.me_ref.refs_0_, bf16[8,3,24,768]{3,2,1,0:T(8,128)(2,1)} %copy-done.6, bf16[8,3,24,768]{3,2,1,0:T(8,128)(2,1)} %copy-done.7, bf16[8,3,24,768]{3,2,1,0:T(8,128)(2,1)} %collective-permute-done.16.refs_2_, ...), custom_call_target="tpu_custom_call" | custom-call | bytes 11796480 | tf_op jit(solution)/shard_map/pallas_call | solution.py:111
  198.4 30.6 %shard_map.318 = (bf16[4,256,768]{2,1,0:T(8,128)(2,1)}, bf16[4,256,768]{2,1,0:T(8,128)(2,1)}, f32[4,256,768]{2,1,0:T(8,128)}, f32[4,256,1]{2,1,0:T(8,128)}, bf16...) custom-call(bf16[4,256,768]{2,1,0:T(8,128)(2,1)} %get-tuple-element., ...), custom_call_target="tpu_custom_call" | custom-call | flops 20000000000 | bytes 40000000 | tf_op jit(solution)/shard_map/pallas_call | solution.py:343
  229.0 10.4 %shard_map.319 = (bf16[16,1,48,768]{3,2,1,0:T(8,128)(2,1)}, bf16[16,1,48,768]{3,2,1,0:T(8,128)(2,1)}, bf16[16,1,48,768]{3,2,1,0:T(8,128)(2,1)}, bf16[16,1,48,768]{3,2,1,0:T(8,128)(2,1)}) custom-call(s32[1]{0:T(128)} %bitcast.me_ref.refs_0_, bf16[4,256,3072]{2,1,0:T(8,128)(2,1)} %get-tuple-element.204.a_ref, bf16[4,256,768]{2,1,0:T(8,128)(2,1)} %get-tuple-element.209.b_ref.e2_ref), custom_call_target="tpu_custom_call" | custom-call | flops 7247757312 | bytes 12582912 | tf_op jit(solution)/shard_map/pallas_call | solution.py:471
  240.0 20.9 %shard_map.320 = (bf16[4,256,3072]{2,1,0:T(8,128)(2,1)}, f32[4,256,768]{2,1,0:T(8,128)}, bf16[4,256,768]{2,1,0:T(8,128)(2,1)}, bf16[4,256,768]{2,1,0:T(8,128)(2,...) custom-call(f32[4,256,768]{2,1,0:T(8,128)} %get-tuple-element.202.dx2_ref, ...), custom_call_target="tpu_custom_call" | custom-call | flops 14000000000 | bytes 50000000 | tf_op jit(solution)/shard_map/pallas_call | solution.py:387
  262.4 4.0 shard_map.321
  266.4 6.5 %shard_map.323 = (bf16[16,2,24,768]{3,2,1,0:T(8,128)(2,1)}, bf16[16,2,24,768]{3,2,1,0:T(8,128)(2,1)}) custom-call(s32[1]{0:T(128)} %bitcast.me_ref.refs_0_, bf16[4,256,768]{2,1,0:T(8,128)(2,1)} %get-tuple-element.222.a_ref, bf16[4,256,3072]{2,1,0:T(8,128)(2,1)} %get-tuple-element.215.b_ref), custom_call_target="tpu_custom_call" | custom-call | flops 3623878656 | bytes 7077888 | tf_op jit(solution)/shard_map/pallas_call | solution.py:439
  272.9 6.6 %shard_map.322 = (bf16[16,2,24,768]{3,2,1,0:T(8,128)(2,1)}, bf16[16,2,24,768]{3,2,1,0:T(8,128)(2,1)}) custom-call(s32[1]{0:T(128)} %bitcast.me_ref.refs_0_, bf16[4,256,768]{2,1,0:T(8,128)(2,1)} %get-tuple-element.222.a_ref, bf16[4,256,3072]{2,1,0:T(8,128)(2,1)} %get-tuple-element.215.b_ref), custom_call_target="tpu_custom_call" | custom-call | flops 3623878656 | bytes 7077888 | tf_op jit(solution)/shard_map/pallas_call | solution.py:439
  279.6 4.6 shard_map.324
  286.8 23.0 %shard_map.325 = (bf16[4,256,256]{2,1,0:T(8,128)(2,1)}, bf16[4,512,256]{2,1,0:T(8,128)(2,1)}, bf16[4,512,256]{2,1,0:T(8,128)(2,1)}, bf16[16,4,24,256]{3,2,1,0:T(...) custom-call(s32[1]{0:T(128)} %bitcast.me_ref.refs_0_, ...), custom_call_target="tpu_custom_call" | custom-call | flops 20000000000 | bytes 30000000 | tf_op jit(solution)/shard_map/pallas_call | solution.py:615
  317.6 4.5 shard_map.327
  324.2 23.3 %shard_map.328 = (bf16[4,256,256]{2,1,0:T(8,128)(2,1)}, bf16[4,512,256]{2,1,0:T(8,128)(2,1)}, bf16[4,512,256]{2,1,0:T(8,128)(2,1)}, bf16[16,4,24,256]{3,2,1,0:T(...) custom-call(s32[1]{0:T(128)} %bitcast.me_ref.refs_0_, ...), custom_call_target="tpu_custom_call" | custom-call | flops 20000000000 | bytes 30000000 | tf_op jit(solution)/shard_map/pallas_call | solution.py:615
  352.2 3.0 shard_map.330
  356.7 23.3 %shard_map.331 = (bf16[4,256,256]{2,1,0:T(8,128)(2,1)}, bf16[4,512,256]{2,1,0:T(8,128)(2,1)}, bf16[4,512,256]{2,1,0:T(8,128)(2,1)}, bf16[16,2,24,256]{3,2,1,0:T(...) custom-call(s32[1]{0:T(128)} %bitcast.me_ref.refs_0_, ...), custom_call_target="tpu_custom_call" | custom-call | flops 20000000000 | bytes 30000000 | tf_op jit(solution)/shard_map/pallas_call | solution.py:615
  383.8 3.2 shard_map.333
  396.8 11.4 %shard_map.336 = bf16[4,512,768]{2,1,0:T(8,128)(2,1)} custom-call(bf16[4,256,256]{2,1,0:T(8,128)(2,1)} %get-tuple-element.239.refs_0_, bf16[4,256,256]{2,1,0:T(8,128)(2,1)} %get-tuple-element.257.refs_1_, bf16[4,256,256]{2,1,0:T(8,128)(2,1)} %get-tuple-element.274.refs_2_, bf16[4,512,256]{2,1,0:T(8,128)(2,1)} %get-tuple-element.275.refs_3_, ...), custom_call_target="tpu_custom_call" | custom-call | flops 10000000000 | bytes 20000000 | tf_op jit(solution)/shard_map/pallas_call | solution.py:651
  430.8 3.6 collective-permute-start.62
  446.4 3.5 collective-permute-start.55
  452.6 12.4 %collective-permute-done.63 = bf16[5,24,256]{1,2,0:T(8,128)(2,1)S(1)} collective-permute-done((bf16[5,24,256]{1,2,0:T(8,128)(2,1)S(1)}, bf16[5,24,256]{1,2,0:T(8,128)(2,1)S(1)}, u32[]{:S(2)}, u32[]{:S(2)}) %collective-permute-start.63) | collective-permute-done | bytes 61472 | tf_op jit(solution)/shard_map/ppermute | solution.py:74
  469.4 4.7 collective-permute-done.56.refs_2_
  474.8 3.1 shard_map.341
  (357 shorter events, 130.6 us)
Async XLA Ops:
  26.6 27.8 %collective-permute-start.3 = (bf16[4,7,24,256]{3,2,1,0:T(8,128)(2,1)S(1)}, bf16[4,7,24,256]{3,2,1,0:T(8,128)(2,1)S(1)}, u32[]{:S(2)}, u32[]{:S(2)}) collective-permute-start(bf16[4,7,24,256]{3,2,1,0:T(8,128)(2,1)S(1)} %pad_maximum_fusion.2), channel_id=1, source_target_pairs={{0,1},{1,0},{2,3},{3,2},{4,5},{5,4},{6,7},{7,6},{8,9},{9,8},{10,11... | collective-permute-start | bytes 1032200 | tf_op jit(solution)/shard_map/ppermute | solution.py:74
  52.1 27.9 %collective-permute-start.8 = (bf16[8,6,24,256]{3,2,1,0:T(8,128)(2,1)S(1)}, bf16[8,6,24,256]{3,2,1,0:T(8,128)(2,1)}, u32[]{:S(2)}, u32[]{:S(2)}) collective-permute-start(bf16[8,6,24,256]{3,2,1,0:T(8,128)(2,1)S(1)} %constant_dynamic-update-slice_fusion.10.refs_4_), channel_id=1, source_target_pairs={{0,1},{1,0},{2,3},{3,2},{4,5},{5,4},{6,7},{7,6},{8,9},{9,8},{10,11... | collective-permute-start | bytes 1769480 | tf_op jit(solution)/shard_map/ppermute | solution.py:74
  53.6 27.9 %collective-permute-start.9 = (bf16[8,6,24,256]{3,2,1,0:T(8,128)(2,1)S(1)}, bf16[8,6,24,256]{3,2,1,0:T(8,128)(2,1)S(1)}, u32[]{:S(2)}, u32[]{:S(2)}) collective-permute-start(bf16[8,6,24,256]{3,2,1,0:T(8,128)(2,1)S(1)} %constant_dynamic-update-slice_fusion.10.refs_4_), channel_id=1, source_target_pairs={{0,4},{1,5},{2,6},{3,7},{4,0},{5,1},{6,2},{7,3},{8,12},{9,13},{10,... | collective-permute-start | bytes 1769480 | tf_op jit(solution)/shard_map/ppermute | solution.py:74
  78.7 31.0 %collective-permute-start.6 = (bf16[8,7,24,256]{3,2,1,0:T(8,128)(2,1)}, bf16[8,7,24,256]{3,2,1,0:T(8,128)(2,1)}, u32[]{:S(2)}, u32[]{:S(2)}) collective-permute-start(bf16[8,7,24,256]{3,2,1,0:T(8,128)(2,1)} %collective-permute-done.4.refs_1_), channel_id=1, source_target_pairs={{0,4},{1,5},{2,6},{3,7},{4,0},{5,1},{6,2},{7,3},{8,12},{9,13},{10,... | collective-permute-start | bytes 2064392 | tf_op jit(solution)/shard_map/ppermute | solution.py:74
  80.0 28.2 %collective-permute-start.30 = (bf16[8,1,48,768]{3,2,1,0:T(8,128)(2,1)}, bf16[8,1,48,768]{3,2,1,0:T(8,128)(2,1)}, u32[]{:S(2)}, u32[]{:S(2)}) collective-permute-start(bf16[8,1,48,768]{3,2,1,0:T(8,128)(2,1)} %constant_dynamic-update-slice_fusion.30.refs_4_), channel_id=1, source_target_pairs={{0,1},{1,0},{2,3},{3,2},{4,5},{5,4},{6,7},{7,6},{8,9},{9,8},{10,11... | collective-permute-start | bytes 1769480 | tf_op jit(solution)/shard_map/ppermute | solution.py:74
  81.5 28.2 %collective-permute-start.10 = (bf16[8,6,24,256]{3,2,1,0:T(8,128)(2,1)}, bf16[8,6,24,256]{3,2,1,0:T(8,128)(2,1)}, u32[]{:S(2)}, u32[]{:S(2)}) collective-permute-start(bf16[8,6,24,256]{3,2,1,0:T(8,128)(2,1)} %collective-permute-done.8.refs_5_), channel_id=1, source_target_pairs={{0,4},{1,5},{2,6},{3,7},{4,0},{5,1},{6,2},{7,3},{8,12},{9,13},{10,... | collective-permute-start | bytes 1769480 | tf_op jit(solution)/shard_map/ppermute | solution.py:74
  81.6 42.4 %collective-permute-start.15 = (bf16[8,3,24,768]{3,2,1,0:T(8,128)(2,1)S(1)}, bf16[8,3,24,768]{3,2,1,0:T(8,128)(2,1)S(1)}, u32[]{:S(2)}, u32[]{:S(2)}) collective-permute-start(bf16[8,3,24,768]{3,2,1,0:T(8,128)(2,1)S(1)} %constant_dynamic-update-slice_fusion.15.refs_0_), channel_id=1, source_target_pairs={{0,2},{1,3},{2,0},{3,1},{4,6},{5,7},{6,4},{7,5},{8,10},{9,11},{10,... | collective-permute-start | bytes 2654216 | tf_op jit(solution)/shard_map/ppermute | solution.py:74
  95.9 25.1 %collective-permute-start.31 = (bf16[8,1,48,768]{3,2,1,0:T(8,128)(2,1)}, bf16[8,1,48,768]{3,2,1,0:T(8,128)(2,1)S(1)}, u32[]{:S(2)}, u32[]{:S(2)}) collective-permute-start(bf16[8,1,48,768]{3,2,1,0:T(8,128)(2,1)} %constant_dynamic-update-slice_fusion.30.refs_4_), channel_id=1, source_target_pairs={{0,4},{1,5},{2,6},{3,7},{4,0},{5,1},{6,2},{7,3},{8,12},{9,13},{10,... | collective-permute-start | bytes 1769480 | tf_op jit(solution)/shard_map/ppermute | solution.py:74
  121.0 71.5 %collective-permute-start.20 = (bf16[8,2,24,768]{3,2,1,0:T(8,128)(2,1)}, bf16[8,2,24,768]{3,2,1,0:T(8,128)(2,1)}, u32[]{:S(2)}, u32[]{:S(2)}) collective-permute-start(bf16[8,2,24,768]{3,2,1,0:T(8,128)(2,1)} %constant_dynamic-update-slice_fusion.20.refs_4_), channel_id=1, source_target_pairs={{0,4},{1,5},{2,6},{3,7},{4,0},{5,1},{6,2},{7,3},{8,12},{9,13},{10,... | collective-permute-start | bytes 1769480 | tf_op jit(solution)/shard_map/ppermute | solution.py:74
  123.4 69.1 %collective-permute-start.16 = (bf16[8,3,24,768]{3,2,1,0:T(8,128)(2,1)S(1)}, bf16[8,3,24,768]{3,2,1,0:T(8,128)(2,1)}, u32[]{:S(2)}, u32[]{:S(2)}) collective-permute-start(bf16[8,3,24,768]{3,2,1,0:T(8,128)(2,1)S(1)} %constant_dynamic-update-slice_fusion.15.refs_0_), channel_id=1, source_target_pairs={{0,4},{1,5},{2,6},{3,7},{4,0},{5,1},{6,2},{7,3},{8,12},{9,13},{10,... | collective-permute-start | bytes 2654216 | tf_op jit(solution)/shard_map/ppermute | solution.py:74
  123.4 69.1 %collective-permute-start.21 = (bf16[8,2,24,768]{3,2,1,0:T(8,128)(2,1)}, bf16[8,2,24,768]{3,2,1,0:T(8,128)(2,1)}, u32[]{:S(2)}, u32[]{:S(2)}) collective-permute-start(bf16[8,2,24,768]{3,2,1,0:T(8,128)(2,1)} %collective-permute-done.19.refs_5_), channel_id=1, source_target_pairs={{0,4},{1,5},{2,6},{3,7},{4,0},{5,1},{6,2},{7,3},{8,12},{9,13},{10,... | collective-permute-start | bytes 1769480 | tf_op jit(solution)/shard_map/ppermute | solution.py:74
  123.9 63.9 %collective-permute-start.28 = (bf16[8,1,48,768]{3,2,1,0:T(8,128)(2,1)}, bf16[8,1,48,768]{3,2,1,0:T(8,128)(2,1)}, u32[]{:S(2)}, u32[]{:S(2)}) collective-permute-start(bf16[8,1,48,768]{3,2,1,0:T(8,128)(2,1)} %collective-permute-done.26.refs_1_), channel_id=1, source_target_pairs={{0,4},{1,5},{2,6},{3,7},{4,0},{5,1},{6,2},{7,3},{8,12},{9,13},{10,... | collective-permute-start | bytes 1769480 | tf_op jit(solution)/shard_map/ppermute | solution.py:74
  124.0 68.5 %collective-permute-start.17 = (bf16[8,3,24,768]{3,2,1,0:T(8,128)(2,1)S(1)}, bf16[8,3,24,768]{3,2,1,0:T(8,128)(2,1)}, u32[]{:S(2)}, u32[]{:S(2)}) collective-permute-start(bf16[8,3,24,768]{3,2,1,0:T(8,128)(2,1)S(1)} %collective-permute-done.15.refs_1_), channel_id=1, source_target_pairs={{0,4},{1,5},{2,6},{3,7},{4,0},{5,1},{6,2},{7,3},{8,12},{9,13},{10,... | collective-permute-start | bytes 2654216 | tf_op jit(solution)/shard_map/ppermute | solution.py:74
  284.1 30.9 %collective-permute-start.38 = (bf16[16,1,24,768]{3,2,1,0:T(8,128)(2,1)}, bf16[16,1,24,768]{3,2,1,0:T(8,128)(2,1)S(1)}, u32[]{:S(2)}, u32[]{:S(2)}) collective-permute-start(bf16[16,1,24,768]{3,2,1,0:T(8,128)(2,1)} %get-tuple-element.230), channel_id=1, source_target_pairs={{0,4},{1,5},{2,6},{3,7},{4,0},{5,1},{6,2},{7,3},{8,12},{9,13},{10,... | collective-permute-start | bytes 1769480 | tf_op jit(solution)/shard_map/ppermute | solution.py:74
  284.2 31.3 %collective-permute-start.39 = (bf16[16,2,24,768]{3,2,1,0:T(8,128)(2,1)}, bf16[16,2,24,768]{3,2,1,0:T(8,128)(2,1)S(1)}, u32[]{:S(2)}, u32[]{:S(2)}) collective-permute-start(bf16[16,2,24,768]{3,2,1,0:T(8,128)(2,1)} %get-tuple-element.226), channel_id=1, source_target_pairs={{0,4},{1,5},{2,6},{3,7},{4,0},{5,1},{6,2},{7,3},{8,12},{9,13},{10,... | collective-permute-start | bytes 3538952 | tf_op jit(solution)/shard_map/ppermute | solution.py:74
  284.6 30.9 %collective-permute-start.37 = (bf16[16,2,24,768]{3,2,1,0:T(8,128)(2,1)S(1)}, bf16[16,2,24,768]{3,2,1,0:T(8,128)(2,1)S(1)}, u32[]{:S(2)}, u32[]{:S(2)}) collective-permute-start(bf16[16,2,24,768]{3,2,1,0:T(8,128)(2,1)S(1)} %copy-done.49), channel_id=1, source_target_pairs={{0,4},{1,5},{2,6},{3,7},{4,0},{5,1},{6,2},{7,3},{8,12},{9,13},{10,... | collective-permute-start | bytes 3538952 | tf_op jit(solution)/shard_map/ppermute | solution.py:74
  284.7 25.1 %collective-permute-start.35 = (bf16[8,1,48,768]{3,2,1,0:T(8,128)(2,1)S(1)}, bf16[8,1,48,768]{3,2,1,0:T(8,128)(2,1)S(1)}, u32[]{:S(2)}, u32[]{:S(2)}) collective-permute-start(bf16[8,1,48,768]{3,2,1,0:T(8,128)(2,1)S(1)} %copy-done.50), channel_id=1, source_target_pairs={{0,2},{1,3},{2,0},{3,1},{4,6},{5,7},{6,4},{7,5},{8,10},{9,11},{10,... | collective-permute-start | bytes 1769480 | tf_op jit(solution)/shard_map/ppermute | solution.py:74
  286.2 23.7 %collective-permute-start.36 = (bf16[8,1,48,768]{3,2,1,0:T(8,128)(2,1)}, bf16[8,1,48,768]{3,2,1,0:T(8,128)(2,1)S(1)}, u32[]{:S(2)}, u32[]{:S(2)}) collective-permute-start(bf16[8,1,48,768]{3,2,1,0:T(8,128)(2,1)} %get-tuple-element.241), channel_id=1, source_target_pairs={{0,1},{1,0},{2,3},{3,2},{4,5},{5,4},{6,7},{7,6},{8,9},{9,8},{10,11... | collective-permute-start | bytes 1769480 | tf_op jit(solution)/shard_map/ppermute | solution.py:74
  309.8 70.7 %collective-permute-start.46 = (bf16[16,4,24,256]{3,2,1,0:T(8,128)(2,1)}, bf16[16,4,24,256]{3,2,1,0:T(8,128)(2,1)S(1)}, u32[]{:S(2)}, u32[]{:S(2)}) collective-permute-start(bf16[16,4,24,256]{3,2,1,0:T(8,128)(2,1)} %get-tuple-element.290), channel_id=1, source_target_pairs={{0,4},{1,5},{2,6},{3,7},{4,0},{5,1},{6,2},{7,3},{8,12},{9,13},{10,... | collective-permute-start | bytes 2359304 | tf_op jit(solution)/shard_map/ppermute | solution.py:74
  313.5 34.0 %collective-permute-start.40 = (bf16[4,1,48,768]{3,2,1,0:T(8,128)(2,1)}, bf16[4,1,48,768]{3,2,1,0:T(8,128)(2,1)S(1)}, u32[]{:S(2)}, u32[]{:S(2)}) collective-permute-start(bf16[4,1,48,768]{3,2,1,0:T(8,128)(2,1)} %get-tuple-element.258), channel_id=1, source_target_pairs={{0,1},{1,0},{2,3},{3,2},{4,5},{5,4},{6,7},{7,6},{8,9},{9,8},{10,11... | collective-permute-start | bytes 884744 | tf_op jit(solution)/shard_map/ppermute | solution.py:74
  315.0 32.5 %collective-permute-start.41 = (bf16[4,1,48,768]{3,2,1,0:T(8,128)(2,1)}, bf16[4,1,48,768]{3,2,1,0:T(8,128)(2,1)S(1)}, u32[]{:S(2)}, u32[]{:S(2)}) collective-permute-start(bf16[4,1,48,768]{3,2,1,0:T(8,128)(2,1)} %get-tuple-element.259), channel_id=1, source_target_pairs={{0,2},{1,3},{2,0},{3,1},{4,6},{5,7},{6,4},{7,5},{8,10},{9,11},{10,... | collective-permute-start | bytes 884744 | tf_op jit(solution)/shard_map/ppermute | solution.py:74
  322.2 28.3 %collective-permute-start.42 = (bf16[8,3,24,768]{3,2,1,0:T(8,128)(2,1)}, bf16[8,3,24,768]{3,2,1,0:T(8,128)(2,1)S(1)}, u32[]{:S(2)}, u32[]{:S(2)}) collective-permute-start(bf16[8,3,24,768]{3,2,1,0:T(8,128)(2,1)} %get-tuple-element.265), channel_id=1, source_target_pairs={{0,2},{1,3},{2,0},{3,1},{4,6},{5,7},{6,4},{7,5},{8,10},{9,11},{10,... | collective-permute-start | bytes 2654216 | tf_op jit(solution)/shard_map/ppermute | solution.py:74
  323.7 26.7 %collective-permute-start.43 = (bf16[8,2,24,768]{3,2,1,0:T(8,128)(2,1)}, bf16[8,2,24,768]{3,2,1,0:T(8,128)(2,1)S(1)}, u32[]{:S(2)}, u32[]{:S(2)}) collective-permute-start(bf16[8,2,24,768]{3,2,1,0:T(8,128)(2,1)} %get-tuple-element.266), channel_id=1, source_target_pairs={{0,1},{1,0},{2,3},{3,2},{4,5},{5,4},{6,7},{7,6},{8,9},{9,8},{10,11... | collective-permute-start | bytes 1769480 | tf_op jit(solution)/shard_map/ppermute | solution.py:74
  347.5 35.4 %collective-permute-start.47 = (bf16[16,4,24,256]{3,2,1,0:T(8,128)(2,1)}, bf16[16,4,24,256]{3,2,1,0:T(8,128)(2,1)S(1)}, u32[]{:S(2)}, u32[]{:S(2)}) collective-permute-start(bf16[16,4,24,256]{3,2,1,0:T(8,128)(2,1)} %get-tuple-element.292), channel_id=1, source_target_pairs={{0,4},{1,5},{2,6},{3,7},{4,0},{5,1},{6,2},{7,3},{8,12},{9,13},{10,... | collective-permute-start | bytes 2359304 | tf_op jit(solution)/shard_map/ppermute | solution.py:74
  355.2 38.5 %collective-permute-start.44 = (bf16[4,3,24,768]{3,2,1,0:T(8,128)(2,1)}, bf16[4,3,24,768]{3,2,1,0:T(8,128)(2,1)S(1)}, u32[]{:S(2)}, u32[]{:S(2)}) collective-permute-start(bf16[4,3,24,768]{3,2,1,0:T(8,128)(2,1)} %get-tuple-element.282), channel_id=1, source_target_pairs={{0,1},{1,0},{2,3},{3,2},{4,5},{5,4},{6,7},{7,6},{8,9},{9,8},{10,11... | collective-permute-start | bytes 1327112 | tf_op jit(solution)/shard_map/ppermute | solution.py:74
  387.0 32.2 %collective-permute-start.68 = (bf16[2,48,768]{2,1,0:T(8,128)(2,1)S(1)}, bf16[2,48,768]{2,1,0:T(8,128)(2,1)S(1)}, u32[]{:S(2)}, u32[]{:S(2)}) collective-permute-start(bf16[2,48,768]{2,1,0:T(8,128)(2,1)S(1)} %copy-done.57), channel_id=1, source_target_pairs={{0,8},{1,9},{2,10},{3,11},{4,12},{5,13},{6,14},{7,15},{8,0},{9,1},... | collective-permute-start | bytes 442376 | tf_op jit(solution)/shard_map/ppermute | solution.py:74
  387.6 26.3 %collective-permute-start.51 = (bf16[8,4,24,256]{3,2,1,0:T(8,128)(2,1)}, bf16[8,4,24,256]{3,2,1,0:T(8,128)(2,1)S(1)}, u32[]{:S(2)}, u32[]{:S(2)}) collective-permute-start(bf16[8,4,24,256]{3,2,1,0:T(8,128)(2,1)} %get-tuple-element.314), channel_id=1, source_target_pairs={{0,2},{1,3},{2,0},{3,1},{4,6},{5,7},{6,4},{7,5},{8,10},{9,11},{10,... | collective-permute-start | bytes 1179656 | tf_op jit(solution)/shard_map/ppermute | solution.py:74
  389.2 25.6 %collective-permute-start.52 = (bf16[8,4,24,256]{3,2,1,0:T(8,128)(2,1)}, bf16[8,4,24,256]{3,2,1,0:T(8,128)(2,1)S(1)}, u32[]{:S(2)}, u32[]{:S(2)}) collective-permute-start(bf16[8,4,24,256]{3,2,1,0:T(8,128)(2,1)} %get-tuple-element.315), channel_id=1, source_target_pairs={{0,1},{1,0},{2,3},{3,2},{4,5},{5,4},{6,7},{7,6},{8,9},{9,8},{10,11... | collective-permute-start | bytes 1179656 | tf_op jit(solution)/shard_map/ppermute | solution.py:74
  435.6 29.4 %collective-permute-start.63 = (bf16[5,24,256]{1,2,0:T(8,128)(2,1)S(1)}, bf16[5,24,256]{1,2,0:T(8,128)(2,1)S(1)}, u32[]{:S(2)}, u32[]{:S(2)}) collective-permute-start(bf16[5,24,256]{1,2,0:T(8,128)(2,1)S(1)} %copy.108), channel_id=1, source_target_pairs={{0,16},{1,17},{2,18},{3,19},{4,20},{5,21},{6,22},{7,23},{8,24},{9,... | collective-permute-start | bytes 184328 | tf_op jit(solution)/shard_map/ppermute | solution.py:74
  435.6 29.4 %collective-permute-start.64 = (bf16[5,24,256]{1,2,0:T(8,128)(2,1)S(1)}, bf16[5,24,256]{1,2,0:T(8,128)(2,1)S(1)}, u32[]{:S(2)}, u32[]{:S(2)}) collective-permute-start(bf16[5,24,256]{1,2,0:T(8,128)(2,1)S(1)} %copy.109), channel_id=1, source_target_pairs={{0,24},{1,25},{2,26},{3,27},{4,28},{5,29},{6,30},{7,31},{8,16},{9,... | collective-permute-start | bytes 184328 | tf_op jit(solution)/shard_map/ppermute | solution.py:74
  449.9 24.2 %collective-permute-start.56 = (bf16[8,24,256]{2,1,0:T(8,128)(2,1)}, bf16[8,24,256]{2,1,0:T(8,128)(2,1)S(1)}, u32[]{:S(2)}, u32[]{:S(2)}) collective-permute-start(bf16[8,24,256]{2,1,0:T(8,128)(2,1)} %get-tuple-element.326), channel_id=1, source_target_pairs={{0,16},{1,17},{2,18},{3,19},{4,20},{5,21},{6,22},{7,23},{8,24},{9,... | collective-permute-start | bytes 294920 | tf_op jit(solution)/shard_map/ppermute | solution.py:74
  451.1 23.1 %collective-permute-start.57 = (bf16[8,24,256]{2,1,0:T(8,128)(2,1)}, bf16[8,24,256]{2,1,0:T(8,128)(2,1)S(1)}, u32[]{:S(2)}, u32[]{:S(2)}) collective-permute-start(bf16[8,24,256]{2,1,0:T(8,128)(2,1)} %get-tuple-element.327), channel_id=1, source_target_pairs={{0,24},{1,25},{2,26},{3,27},{4,28},{5,29},{6,30},{7,31},{8,16},{9,... | collective-permute-start | bytes 294920 | tf_op jit(solution)/shard_map/ppermute | solution.py:74
  (98 other events, 1087.4 us)
